TPU v7x, 128 devices: a whole 4x4x4 slice. The times are simulated.
128 devices in a mesh: dp: 2 (over x_hi), ctx: 64 (over y, x_lo, z, core).
Axes of the slice: x: 4 (x_hi: 2, x_lo: 2; x = x_hi * 2 + x_lo), y: 4, z: 4, core: 2. Of those that a mesh axis runs over, the one named last changes fastest.
Arguments:
- queries: bfloat16 [40960, 3072], P(('dp', 'ctx')), parts along dimension 0, may hold values from -300 to 300
- latent: bfloat16 [40960, 576], P(('dp', 'ctx')), parts along dimension 0, may hold values from -4 to 4
- w_key_up: bfloat16 [512, 2048], replicated, may hold values from -0.25 to 0.25
- w_value_up: bfloat16 [512, 2048], replicated, may hold values from -0.25 to 0.25
- grad_out: bfloat16 [40960, 2048], P(('dp', 'ctx')), parts along dimension 0, may hold values from -6 to 6
- span_order: int32 [256], P('dp'), parts along dimension 0, may hold values from 0 to 127, each once
Outputs:
- attn_out: bfloat16 [40960, 2048], P(('dp', 'ctx')), parts along dimension 0
- grad_queries: bfloat16 [40960, 3072], P(('dp', 'ctx')), parts along dimension 0
- grad_latent: bfloat16 [40960, 576], P(('dp', 'ctx')), parts along dimension 0
There are 2 independent parts, one for each index of `dp`. A program takes and returns all parts, laid end to end along the dimension named above; an argument that names none is the same for every part. Nothing has to cross between parts.
Inputs may be any that keep to these rules, and one draw needn't show every extreme that they name: `span_order`: each block number appears once.
All inputs are finite; a program needn't handle non-finite values.
Results may differ from a plain program's by a relative error of at most 0.0083.
Values may be sent and summed in bfloat16 or wider, within the bound.
No kernel may reach another device: no remote copies, remote signals or barrier semaphores. Data moves between devices by JAX's collectives and lax.ppermute only.
A program may use at most 192 MiB of HBM per device.

v0:
```python
import jax
import jax.numpy as jnp
from jax import lax
from jax.experimental import pallas as pl
from jax.experimental.pallas import tpu as pltpu
from jax.sharding import PartitionSpec as P
HEADS=16; NOPE=128; ROPE=64; VDIM=128; LATENT=512; DQ=192
SCALE=DQ**-0.5
C2=SCALE*1.4426950408889634
NEG=-1e30
NT=(((1,),(1,)),((),()))
TN=(((0,),(0,)),((),()))
F32=jnp.float32; BF=jnp.bfloat16

def body(spans, q_ref, do_ref, own, near, far, wk_ref, wv_ref, out_ref, dq_ref, t_ref, bias, lat, rope, accT, ropeT):
    p=pl.program_id(0)
    T=q_ref.shape[0]; W=3*T; H=T//2
    @pl.when(p==0)
    def _():
        lat[0:T]=own[:, :LATENT]; lat[T:2*T]=near[:, :LATENT]; lat[2*T:]=far[:, :LATENT]
        rope[0:T]=own[:, LATENT:]; rope[T:2*T]=near[:, LATENT:]; rope[2*T:]=far[:, LATENT:]
        col=lax.broadcasted_iota(jnp.int32,(1,W),1)
        kp=jnp.full((1,W),spans[5]*H-5*H,jnp.int32)
        for j in range(4,-1,-1):
            kp=jnp.where(col<(j+1)*H, spans[j]*H-j*H, kp)
        kp=kp+col
        row=lax.broadcasted_iota(jnp.int32,(T,1),0)
        qp=jnp.where(row<H, spans[0]*H, spans[1]*H-H)+row
        bias[...]=jnp.where(kp<=qp,0.0,NEG).astype(F32)
        accT[...]=jnp.zeros_like(accT); ropeT[...]=jnp.zeros_like(ropeT)
    outs=[];dqs=[];dks=[];dvs=[]; rt=None
    for h in range(2):
        q=q_ref[:, h*DQ:(h+1)*DQ]
        do=do_ref[:, h*VDIM:(h+1)*VDIM]
        w=jnp.concatenate([wk_ref[:, h*128:(h+1)*128], wv_ref[:, h*128:(h+1)*128]],1)
        kv=jnp.dot(lat[...],w,preferred_element_type=F32).astype(BF)
        k=jnp.concatenate([kv[:, :128],rope[...]],1)
        v=kv[:,128:]
        s=lax.dot_general(q,k,NT,preferred_element_type=F32)+bias[...]
        m=jnp.max(s,1,keepdims=True)
        e=jnp.exp2((s-m)*C2).astype(BF)
        va=jnp.concatenate([v,jnp.ones_like(v)],1)
        oa=jnp.dot(e,va,preferred_element_type=F32)
        rl=1.0/oa[:,128:]
        out=oa[:,:128]*rl
        dof=do.astype(F32)
        delta=jnp.sum(out*dof,1,keepdims=True)
        dp=lax.dot_general(do,v,NT,preferred_element_type=F32)
        ds=(e.astype(F32)*(dp-delta)).astype(BF)
        rs=rl[:, :1]*SCALE
        dq=jnp.dot(ds,k,preferred_element_type=F32)*rs
        qs=(q.astype(F32)*rs).astype(BF)
        dos=(dof*rl).astype(BF)
        dk=lax.dot_general(qs,ds,TN,preferred_element_type=F32)
        dv=lax.dot_general(dos,e,TN,preferred_element_type=F32)
        outs.append(out.astype(BF)); dqs.append(dq.astype(BF))
        dks.append(dk[:128].astype(BF)); dvs.append(dv.astype(BF))
        rt=dk[128:] if rt is None else rt+dk[128:]
    out_ref[...]=jnp.concatenate(outs,1)
    dq_ref[...]=jnp.concatenate(dqs,1)
    ropeT[...]+=rt
    wcat=jnp.concatenate([wk_ref[...],wv_ref[...]],1)
    d=jnp.concatenate(dks+dvs,0)
    accT[...]+=jnp.dot(wcat,d,preferred_element_type=F32)
    @pl.when(p==pl.num_programs(0)-1)
    def _():
        t_ref[:, :LATENT]=accT[...].T
        t_ref[:, LATENT:]=ropeT[...].T

def fused(spans,q,do,own,near,far,wk,wv):
    T=q.shape[0]
    full=lambda a: pl.BlockSpec(a.shape,lambda p,s:(0,0))
    col=lambda n: pl.BlockSpec((T,n),lambda p,s:(0,p))
    wsp=pl.BlockSpec((LATENT,256),lambda p,s:(0,p))
    return pl.pallas_call(body,
        grid_spec=pltpu.PrefetchScalarGridSpec(num_scalar_prefetch=1,grid=(HEADS//2,),
          in_specs=[col(384),col(256),full(own),full(near),full(far),wsp,wsp],
          out_specs=[col(256),col(384),pl.BlockSpec((3*T,576),lambda p,s:(0,0))],
          scratch_shapes=[pltpu.VMEM((T,3*T),F32),pltpu.VMEM((3*T,LATENT),BF),pltpu.VMEM((3*T,ROPE),BF),pltpu.VMEM((LATENT,3*T),F32),pltpu.VMEM((ROPE,3*T),F32)]),
        out_shape=[jax.ShapeDtypeStruct((T,2048),BF),jax.ShapeDtypeStruct((T,3072),BF),jax.ShapeDtypeStruct((3*T,576),F32)],
        compiler_params=pltpu.CompilerParams(vmem_limit_bytes=56*2**20,dimension_semantics=("arbitrary",)),
    )(spans,q,do,own,near,far,wk,wv)


def shifted(block, distance):
    n=lax.axis_size("ctx")
    return lax.ppermute(block,"ctx",[((i-distance)%n,i) for i in range(n)])

def on_device(queries, latent, w_key_up, w_value_up, grad_out, span_order):
    n=lax.axis_size("ctx"); me=lax.axis_index("ctx"); T=queries.shape[0]
    near=shifted(latent,1); far=shifted(latent,2)
    pairs=span_order.reshape(n,2)
    spans=jnp.concatenate([pairs[(me-d)%n] for d in range(3)])
    out,dq,t=fused(spans,queries,grad_out,latent,near,far,w_key_up,w_value_up)
    a=shifted(t[T:2*T].astype(BF),-1); b=shifted(t[2*T:].astype(BF),-2)
    total=t[:T]+a.astype(F32)+b.astype(F32)
    return out,dq,total.astype(BF)

def solution(mesh):
    rows=P(("dp","ctx"),None)
    return jax.shard_map(on_device,mesh=mesh,in_specs=(rows,rows,P(),P(),rows,P("dp")),out_specs=(rows,rows,rows),check_vma=False)
```

profile of v0, /device:TPU:0, one launch (start us, length us, event | category | flops | bytes accessed | tf_op | source)
XLA Modules:
  0.0 88.8 jit_solution(3612126998658944928)
XLA Ops:
  0.6 0.1 collective-permute-start
  0.7 2.1 %collective-permute-start.1 = (bf16[320,576]{1,0:T(8,128)(2,1)}, bf16[320,576]{1,0:T(8,128)(2,1)S(1)}, u32[]{:S(2)}, u32[]{:S(2)}) collective-permute-start(bf16[320,576]{1,0:T(8,128)(2,1)} %own.1), channel_id=1, source_target_pairs={{62,0},{63,1},{0,2},{1,3},{2,4},{3,5},{4,6},{5,7},{6,8},{7,9},{8,1... | collective-permute-start | bytes 1105928 | tf_op jit(solution)/shard_map/ppermute | solution.py:87
  2.8 0.8 reshape.9
  3.6 0.6 pad_add_fusion.spans
  4.3 12.7 %collective-permute-done.near = bf16[320,576]{1,0:T(8,128)(2,1)S(1)} collective-permute-done((bf16[320,576]{1,0:T(8,128)(2,1)}, bf16[320,576]{1,0:T(8,128)(2,1)S(1)}, u32[]{:S(2)}, u32[]{:S(2)}) %collective-permute-start) | collective-permute-done | bytes 368672 | tf_op jit(solution)/shard_map/ppermute | solution.py:87
  16.9 0.0 copy-start
  16.9 1.9 %collective-permute-done.1.far = bf16[320,576]{1,0:T(8,128)(2,1)S(1)} collective-permute-done((bf16[320,576]{1,0:T(8,128)(2,1)}, bf16[320,576]{1,0:T(8,128)(2,1)S(1)}, u32[]{:S(2)}, u32[]{:S(2)}) %collective-permute-start.1) | collective-permute-done | bytes 368672 | tf_op jit(solution)/shard_map/ppermute | solution.py:87
  18.8 0.0 copy-done
  18.8 0.0 copy-start.1
  18.8 0.7 copy-done.1
  19.6 46.1 %shard_map.85 = (bf16[320,2048]{1,0:T(8,128)(2,1)}, bf16[320,3072]{1,0:T(8,128)(2,1)}, f32[960,576]{1,0:T(8,128)}) custom-call(s32[6]{0:T(128)} %pad_add_fusion.spans, bf16[320,3072]{1,0:T(8,128)(2,1)} %q_ref.1, bf16[320,2048]{1,0:T(8,128)(2,1)} %do_ref.1, bf16[320,576]{1,0:T(8,128)(2,1)} %own.1, bf16[320,576]{1,0:T(8,128)(2,1)} %copy-done, ...), custom_call_target="tpu_custom_call" | custom-call | tf_op jit(solution)/shard_map/pallas_call | solution.py:75
  65.6 1.8 %convert.4 = bf16[960,576]{1,0:T(8,128)(2,1)S(1)} convert(f32[960,576]{1,0:T(8,128)} %get-tuple-element.8) | non-fusion elementwise | flops 552960 | bytes 3317760 | tf_op jit(solution)/shard_map/convert.1
  67.5 0.1 fusion.3
  67.5 5.3 %collective-permute-start.2 = (bf16[320,576]{1,0:T(8,128)(2,1)S(1)}, bf16[320,576]{1,0:T(8,128)(2,1)S(1)}, u32[]{:S(2)}, u32[]{:S(2)}) collective-permute-start(bf16[320,576]{1,0:T(8,128)(2,1)S(1)} %get-tuple-element.9), channel_id=1, source_target_pairs={{1,0},{2,1},{3,2},{4,3},{5,4},{6,5},{7,6},{8,7},{9,8},{10,9},{11,1... | collective-permute-start | bytes 1105928 | tf_op jit(solution)/shard_map/ppermute | solution.py:87
  72.8 0.4 collective-permute-start.3
  73.2 9.0 %collective-permute-done.2 = bf16[320,576]{1,0:T(8,128)(2,1)S(1)} collective-permute-done((bf16[320,576]{1,0:T(8,128)(2,1)S(1)}, bf16[320,576]{1,0:T(8,128)(2,1)S(1)}, u32[]{:S(2)}, u32[]{:S(2)}) %collective-permute-start.2) | collective-permute-done | bytes 368672 | tf_op jit(solution)/shard_map/ppermute | solution.py:87
  82.2 4.6 %collective-permute-done.3 = bf16[320,576]{1,0:T(8,128)(2,1)S(1)} collective-permute-done((bf16[320,576]{1,0:T(8,128)(2,1)S(1)}, bf16[320,576]{1,0:T(8,128)(2,1)S(1)}, u32[]{:S(2)}, u32[]{:S(2)}) %collective-permute-start.3) | collective-permute-done | bytes 368672 | tf_op jit(solution)/shard_map/ppermute | solution.py:87
  86.7 2.0 %add_convert_fusion = bf16[320,576]{1,0:T(8,128)(2,1)} fusion(bf16[320,576]{1,0:T(8,128)(2,1)S(1)} %collective-permute-done.3, bf16[320,576]{1,0:T(8,128)(2,1)S(1)} %collective-permute-done.2, f32[960,576]{1,0:T(8,128)} %get-tuple-element.8), kind=kLoop, calls=%fused_computation | loop fusion | flops 921600 | bytes 1843200 | tf_op jit(solution)/shard_map/convert_element_type | solution.py:97
  (1 shorter events, 0.0 us)
Async XLA Ops:
  0.6 16.3 %collective-permute-start = (bf16[320,576]{1,0:T(8,128)(2,1)}, bf16[320,576]{1,0:T(8,128)(2,1)S(1)}, u32[]{:S(2)}, u32[]{:S(2)}) collective-permute-start(bf16[320,576]{1,0:T(8,128)(2,1)} %own.1), channel_id=1, source_target_pairs={{63,0},{0,1},{1,2},{2,3},{3,4},{4,5},{5,6},{6,7},{7,8},{8,9},{9,10... | collective-permute-start | bytes 1105928 | tf_op jit(solution)/shard_map/ppermute | solution.py:87
  0.7 18.1 %collective-permute-start.1 = (bf16[320,576]{1,0:T(8,128)(2,1)}, bf16[320,576]{1,0:T(8,128)(2,1)S(1)}, u32[]{:S(2)}, u32[]{:S(2)}) collective-permute-start(bf16[320,576]{1,0:T(8,128)(2,1)} %own.1), channel_id=1, source_target_pairs={{62,0},{63,1},{0,2},{1,3},{2,4},{3,5},{4,6},{5,7},{6,8},{7,9},{8,1... | collective-permute-start | bytes 1105928 | tf_op jit(solution)/shard_map/ppermute | solution.py:87
  16.9 1.9 %copy-start = (bf16[320,576]{1,0:T(8,128)(2,1)}, bf16[320,576]{1,0:T(8,128)(2,1)S(1)}, u32[]{:S(2)}) copy-start(bf16[320,576]{1,0:T(8,128)(2,1)S(1)} %collective-permute-done.near) | copy-start | bytes 1105924
  18.8 0.7 copy-start.1
  67.5 14.6 %collective-permute-start.2 = (bf16[320,576]{1,0:T(8,128)(2,1)S(1)}, bf16[320,576]{1,0:T(8,128)(2,1)S(1)}, u32[]{:S(2)}, u32[]{:S(2)}) collective-permute-start(bf16[320,576]{1,0:T(8,128)(2,1)S(1)} %get-tuple-element.9), channel_id=1, source_target_pairs={{1,0},{2,1},{3,2},{4,3},{5,4},{6,5},{7,6},{8,7},{9,8},{10,9},{11,1... | collective-permute-start | bytes 1105928 | tf_op jit(solution)/shard_map/ppermute | solution.py:87
  72.8 13.9 %collective-permute-start.3 = (bf16[320,576]{1,0:T(8,128)(2,1)S(1)}, bf16[320,576]{1,0:T(8,128)(2,1)S(1)}, u32[]{:S(2)}, u32[]{:S(2)}) collective-permute-start(bf16[320,576]{1,0:T(8,128)(2,1)S(1)} %get-tuple-element.10), channel_id=1, source_target_pairs={{2,0},{3,1},{4,2},{5,3},{6,4},{7,5},{8,6},{9,7},{10,8},{11,9},{12,... | collective-permute-start | bytes 1105928 | tf_op jit(solution)/shard_map/ppermute | solution.py:87
where the time goes:
time: 89 us; the launch traced here: 88.8 us
  Pallas kernels  46.1 us (52%)
  waiting for transfers between devices  28.1 us (32%)
  starting transfers between devices  7.8 us (9%)
  other arithmetic  4.49 us (5%)
  local copies, waits for them, and re-layouts  1.62 us (2%)
    pallas_call x1, Pallas kernels, fused(): pl.pallas_call(body, grid_spec=pltpu.PrefetchScalarGridSpec(num_scalar_pr...  46.1 us
    ppermute x4, waiting for transfers between devices, shifted(): lax.ppermute(block, 'ctx', [((i - distance) % n, i) for i in range(n)])  28.1 us
    ppermute x4, starting transfers between devices, shifted(): lax.ppermute(block, 'ctx', [((i - distance) % n, i) for i in range(n)])  7.8 us
    convert_element_type x1, other arithmetic, on_device(): return (out, dq, total.astype(BF))  2.02 us
    another operation x1, other arithmetic  1.82 us
  transfers between devices with their start and end apart: 4, of which 4 were waited for; matrix products, arithmetic and copies ran while one was open for 2% of the time, Pallas kernels for 0%

commit v1 on v0

v1 whole, which is shorter than its diff:
```python
import jax
import jax.numpy as jnp
from jax import lax
from jax.experimental import pallas as pl
from jax.experimental.pallas import tpu as pltpu
from jax.sharding import PartitionSpec as P

HEADS = 16
NOPE = 128
ROPE = 64
VDIM = 128
LATENT = 512
DQ = NOPE + ROPE
SCALE = DQ**-0.5
EXP2_SCALE = SCALE * 1.4426950408889634
MASKED = -1e30
NT = (((1,), (1,)), ((), ()))
TN = (((0,), (0,)), ((), ()))
F32 = jnp.float32
BF = jnp.bfloat16


def dot(x, y):
    return jnp.dot(x, y, preferred_element_type=F32)


def dot_rows(x, y):
    half = x.shape[0] // 2
    return jnp.concatenate([dot(x[:half], y), dot(x[half:], y)], 0)


def dot_nt(x, y):
    return lax.dot_general(x, y, NT, preferred_element_type=F32)


def dot_tn(x, y):
    return lax.dot_general(x, y, TN, preferred_element_type=F32)


def q_head(ref, h):
    return ref[:, h * DQ : (h + 1) * DQ]


def v_head(ref, h):
    return ref[:, h * VDIM : (h + 1) * VDIM]


def head_weights(wk_ref, wv_ref, h):
    return jnp.concatenate([v_head(wk_ref, h), v_head(wv_ref, h)], 1)


def positions(rows, spans):
    half = rows // 2
    last = len(spans) - 1
    col = lax.broadcasted_iota(jnp.int32, (1, half * len(spans)), 1)
    base = jnp.full(col.shape, (spans[last] - last) * half, jnp.int32)
    for j in range(last - 1, -1, -1):
        base = jnp.where(col < (j + 1) * half, (spans[j] - j) * half, base)
    return base + col


def own_keys(own, wk_ref, wv_ref, kv_ref):
    for h in range(2):
        kv_ref[h] = dot_rows(own[:, :LATENT], head_weights(wk_ref, wv_ref, h)).astype(BF)


def main_body(spans, q_ref, do_ref, own, near, far, wk_ref, wv_ref, okv_ref,
              out_ref, ds_ref, oe_ref, k_ref, dos_ref, tn_ref, tf_ref, bias, acc_t, rope_t):
    p = pl.program_id(0)
    rows = q_ref.shape[0]
    half = rows // 2
    width = 2 * rows
    others = [spans[j] for j in range(2, 6)]
    pair = [spans[0], spans[1]]

    @pl.when(p == 0)
    def _():
        row = lax.broadcasted_iota(jnp.int32, (rows, 1), 0)
        q_pos = jnp.where(row < half, pair[0] * half, (pair[1] - 1) * half) + row
        bias[...] = jnp.where(positions(rows, pair) <= q_pos, 0.0, MASKED).astype(F32)
        acc_t[...] = jnp.zeros_like(acc_t)
        rope_t[...] = jnp.zeros_like(rope_t)

    other_pos = positions(rows, others)
    other_bias = [jnp.where(other_pos < pair[j] * half, 0.0, MASKED).astype(F32) for j in range(2)]
    rope = jnp.concatenate([near[:, LATENT:], far[:, LATENT:], own[:, LATENT:]], 0)

    def project(h):
        w = head_weights(wk_ref, wv_ref, h)
        kv = jnp.concatenate(
            [dot(near[:, :LATENT], w).astype(BF), dot(far[:, :LATENT], w).astype(BF), okv_ref[h]], 0
        )
        k = kv[:, :NOPE]
        k_ref[h] = k
        return jnp.concatenate([k, rope], 1), kv[:, NOPE:]

    def score(h, k):
        return dot_nt(q_head(q_ref, h), k)

    def soften(s):
        upper = s[:half, :width] + other_bias[0]
        lower = s[half:, :width] + other_bias[1]
        s = jnp.concatenate([jnp.concatenate([upper, lower], 0), s[:, width:] + bias[...]], 1)
        top = jnp.max(s, 1, keepdims=True)
        return jnp.exp2((s - top) * EXP2_SCALE).astype(BF)

    def attend(h, e, v):
        oe_ref[h] = e[:, width:]
        both = dot_rows(e, jnp.concatenate([v, jnp.ones_like(v)], 1))
        inv = 1.0 / both[:, VDIM:]
        out = both[:, :VDIM] * inv
        out_ref[:, h * VDIM : (h + 1) * VDIM] = out.astype(BF)
        dos = (v_head(do_ref, h).astype(F32) * inv).astype(BF)
        dos_ref[:, h * VDIM : (h + 1) * VDIM] = dos
        return dos, jnp.sum(out * dos.astype(F32), 1, keepdims=True)

    def dscores(h, e, dp, delta):
        ds = (e.astype(F32) * (dp - delta)).astype(BF)
        ds_ref[h] = ds
        return ds

    k0, v0 = project(0)
    s0 = score(0, k0)
    k1, v1 = project(1)
    e0 = soften(s0)
    s1 = score(1, k1)
    dos0, delta0 = attend(0, e0, v0)
    e1 = soften(s1)
    dp0 = dot_nt(dos0, v0)
    dos1, delta1 = attend(1, e1, v1)
    ds0 = dscores(0, e0, dp0, delta0)
    dp1 = dot_nt(dos1, v1)
    dv0 = dot_tn(dos0, e0[:, :width])
    dk0 = dot_tn(q_head(q_ref, 0), ds0[:, :width]) * SCALE
    ds1 = dscores(1, e1, dp1, delta1)
    dv1 = dot_tn(dos1, e1[:, :width])
    dk1 = dot_tn(q_head(q_ref, 1), ds1[:, :width]) * SCALE
    rope_t[...] += dk0[NOPE:] + dk1[NOPE:]
    w = jnp.concatenate([wk_ref[...], wv_ref[...]], 1)
    d = jnp.concatenate([dk0[:NOPE].astype(BF), dk1[:NOPE].astype(BF), dv0.astype(BF), dv1.astype(BF)], 0)
    acc_t[...] += dot(w, d)

    @pl.when(p == pl.num_programs(0) - 1)
    def _():
        tn_ref[:, :LATENT] = acc_t[:, :rows].astype(BF).T
        tn_ref[:, LATENT:] = rope_t[:, :rows].astype(BF).T
        tf_ref[:, :LATENT] = acc_t[:, rows:].astype(BF).T
        tf_ref[:, LATENT:] = rope_t[:, rows:].astype(BF).T


def tail_body(q_ref, dos_ref, own, near, far, wk_ref, wv_ref, ds_ref, oe_ref, k_ref,
              dq_ref, t_ref, acc_t, rope_t):
    p = pl.program_id(0)
    rows = q_ref.shape[0]
    width = 2 * rows

    @pl.when(p == 0)
    def _():
        acc_t[...] = jnp.zeros_like(acc_t)
        rope_t[...] = jnp.zeros_like(rope_t)

    rope = jnp.concatenate([near[:, LATENT:], far[:, LATENT:], own[:, LATENT:]], 0)
    dqs, dks, dvs, rope_sum = [], [], [], None
    for h in range(2):
        ds = ds_ref[h]
        dv = dot_tn(v_head(dos_ref, h), oe_ref[h])
        dk = dot_tn(q_head(q_ref, h), ds[:, width:]) * SCALE
        dq = dot_rows(ds, jnp.concatenate([k_ref[h], rope], 1)) * SCALE
        dqs.append(dq.astype(BF))
        dks.append(dk[:NOPE].astype(BF))
        dvs.append(dv.astype(BF))
        rope_sum = dk[NOPE:] if rope_sum is None else rope_sum + dk[NOPE:]
    dq_ref[...] = jnp.concatenate(dqs, 1)
    rope_t[...] += rope_sum
    w = jnp.concatenate([wk_ref[...], wv_ref[...]], 1)
    acc_t[...] += dot(w, jnp.concatenate(dks + dvs, 0))

    @pl.when(p == pl.num_programs(0) - 1)
    def _():
        t_ref[:, :LATENT] = acc_t[...].T
        t_ref[:, LATENT:] = rope_t[...].T


def whole(a):
    return pl.BlockSpec(a.shape, lambda p, *_: (0, 0))


def columns(rows, n):
    return pl.BlockSpec((rows, n), lambda p, *_: (0, p))


def pairs(rows, n):
    return pl.BlockSpec((2, rows, n), lambda p, *_: (p, 0, 0))


def params():
    return pltpu.CompilerParams(vmem_limit_bytes=48 * 2**20, dimension_semantics=("arbitrary",))


def cost(macs, size):
    return pl.CostEstimate(flops=2 * macs, bytes_accessed=size, transcendentals=0)


def shape(*dims, dtype=BF):
    return jax.ShapeDtypeStruct(dims, dtype)


def call_own_keys(own, wk, wv):
    rows = own.shape[0]
    return pl.pallas_call(
        own_keys,
        grid=(HEADS // 2,),
        in_specs=[whole(own), columns(LATENT, 256), columns(LATENT, 256)],
        out_specs=pairs(rows, 256),
        out_shape=shape(HEADS, rows, 256),
        compiler_params=params(),
        cost_estimate=cost(7 * 10**8, 8 * 10**6),
        name="own_keys",
    )(own, wk, wv)


def call_main(spans, q, do, own, near, far, wk, wv, okv):
    rows = q.shape[0]
    keys = 3 * rows
    return pl.pallas_call(
        main_body,
        grid_spec=pltpu.PrefetchScalarGridSpec(
            num_scalar_prefetch=1,
            grid=(HEADS // 2,),
            in_specs=[columns(rows, 2 * DQ), columns(rows, 2 * VDIM), whole(own), whole(near), whole(far),
                      columns(LATENT, 256), columns(LATENT, 256), pairs(rows, 256)],
            out_specs=[columns(rows, 2 * VDIM), pairs(rows, keys), pairs(rows, rows), pairs(keys, NOPE),
                       columns(rows, 2 * VDIM), whole(near), whole(far)],
            scratch_shapes=[
                pltpu.VMEM((rows, rows), F32),
                pltpu.VMEM((LATENT, 2 * rows), F32),
                pltpu.VMEM((ROPE, 2 * rows), F32),
            ],
        ),
        out_shape=[
            shape(*do.shape),
            shape(HEADS, rows, keys),
            shape(HEADS, rows, rows),
            shape(HEADS, keys, NOPE),
            shape(*do.shape),
            shape(*near.shape),
            shape(*far.shape),
        ],
        compiler_params=params(),
        cost_estimate=cost(9 * 10**9, 35 * 10**6),
        name="attend_main",
    )(spans, q, do, own, near, far, wk, wv, okv)


def call_tail(q, dos, own, near, far, wk, wv, ds, oe, k):
    rows = q.shape[0]
    keys = 3 * rows
    return pl.pallas_call(
        tail_body,
        grid=(HEADS // 2,),
        in_specs=[columns(rows, 2 * DQ), columns(rows, 2 * VDIM), whole(own), whole(near), whole(far),
                  columns(LATENT, 256), columns(LATENT, 256),
                  pairs(rows, keys), pairs(rows, rows), pairs(keys, NOPE)],
        out_specs=[columns(rows, 2 * DQ), whole(own)],
        scratch_shapes=[pltpu.VMEM((LATENT, rows), F32), pltpu.VMEM((ROPE, rows), F32)],
        out_shape=[shape(*q.shape), shape(*own.shape, dtype=F32)],
        compiler_params=params(),
        cost_estimate=cost(4 * 10**9, 30 * 10**6),
        name="attend_tail",
    )(q, dos, own, near, far, wk, wv, ds, oe, k)


def shifted(block, distance):
    n = lax.axis_size("ctx")
    return lax.ppermute(block, "ctx", [((i - distance) % n, i) for i in range(n)])


def on_device(queries, latent, w_key_up, w_value_up, grad_out, span_order):
    n = lax.axis_size("ctx")
    me = lax.axis_index("ctx")
    near = shifted(latent, 1)
    far = shifted(latent, 2)
    order = span_order.reshape(n, 2)
    spans = jnp.concatenate([order[(me - lag) % n] for lag in range(3)])
    okv = call_own_keys(latent, w_key_up, w_value_up)
    out, ds, oe, k, dos, t_near, t_far = call_main(
        spans, queries, grad_out, latent, near, far, w_key_up, w_value_up, okv
    )
    from_far = shifted(t_far, -2)
    from_near = shifted(t_near, -1)
    dq, own_term = call_tail(queries, dos, latent, near, far, w_key_up, w_value_up, ds, oe, k)
    total = own_term + from_near.astype(F32) + from_far.astype(F32)
    return out, dq, total.astype(BF)


def solution(mesh):
    rows = P(("dp", "ctx"), None)
    return jax.shard_map(
        on_device,
        mesh=mesh,
        in_specs=(rows, rows, P(), P(), rows, P("dp")),
        out_specs=(rows, rows, rows),
        check_vma=False,
    )
```

time: 89 us -> 71 us (0.80)
  the two profiles are of different devices: /device:TPU:0 before, /device:TPU:1 now
where the time goes in v1:
time: 71 us; the launch traced here: 70.6 us
  Pallas kernels  49.6 us (70%)
  starting transfers between devices  12.1 us (17%)
  local copies, waits for them, and re-layouts  4.99 us (7%)
  waiting for transfers between devices  2.28 us (3%)
  other arithmetic  0.95 us (1%)
    pallas_call x1, Pallas kernels, call_main(): pl.pallas_call(main_body, grid_spec=pltpu.PrefetchScalarGridSpec(num_scal...  30 us
    pallas_call x1, Pallas kernels, call_tail(): pl.pallas_call(tail_body, grid=(HEADS // 2,), in_specs=[columns(rows, 2 *...  14.5 us
    ppermute x4, starting transfers between devices, shifted(): lax.ppermute(block, 'ctx', [((i - distance) % n, i) for i in range(n)])  12.1 us
    pallas_call x1, Pallas kernels, call_own_keys(): pl.pallas_call(own_keys, grid=(HEADS // 2,), in_specs=[whole(own), column...  5.06 us
    unnamed x10, local copies, waits for them, and re-layouts  4.19 us
    ppermute x4, waiting for transfers between devices, shifted(): lax.ppermute(block, 'ctx', [((i - distance) % n, i) for i in range(n)])  2.28 us
  transfers between devices with their start and end apart: 4, of which 1 were waited for; matrix products, arithmetic and copies ran while one was open for 1% of the time, Pallas kernels for 28%

profile of v1, /device:TPU:1, one launch (start us, length us, event | category | flops | bytes accessed | tf_op | source)
XLA Modules:
  0.0 70.6 jit_solution(5837673649688291525)
XLA Ops:
  0.6 2.5 %collective-permute-start.1 = (bf16[320,576]{1,0:T(8,128)(2,1)}, bf16[320,576]{1,0:T(8,128)(2,1)S(1)}, u32[]{:S(2)}, u32[]{:S(2)}) collective-permute-start(bf16[320,576]{1,0:T(8,128)(2,1)} %own.5), channel_id=1, source_target_pairs={{62,0},{63,1},{0,2},{1,3},{2,4},{3,5},{4,6},{5,7},{6,8},{7,9},{8,1... | collective-permute-start | bytes 1105928 | tf_op jit(solution)/shard_map/ppermute | solution.py:275
  3.2 2.5 %collective-permute-start = (bf16[320,576]{1,0:T(8,128)(2,1)}, bf16[320,576]{1,0:T(8,128)(2,1)S(1)}, u32[]{:S(2)}, u32[]{:S(2)}) collective-permute-start(bf16[320,576]{1,0:T(8,128)(2,1)} %own.5), channel_id=1, source_target_pairs={{63,0},{0,1},{1,2},{2,3},{3,4},{4,5},{5,6},{6,7},{7,8},{8,9},{9,10... | collective-permute-start | bytes 1105928 | tf_op jit(solution)/shard_map/ppermute | solution.py:275
  5.6 0.8 %reshape.9 = s32[64,2]{1,0:T(8,128)S(1)} reshape(s32[128]{0:T(128)} %param.11) | data formatting | bytes 1024 | tf_op jit(solution)/shard_map/reshape | solution.py:283
  6.5 0.1 pad_add_fusion.spans
  6.5 0.0 copy-start
  6.6 1.6 %copy-done = bf16[512,2048]{1,0:T(8,128)(2,1)S(1)} copy-done((bf16[512,2048]{1,0:T(8,128)(2,1)S(1)}, bf16[512,2048]{1,0:T(8,128)(2,1)}, u32[]{:S(2)}) %copy-start) | copy-done | bytes 2097176
  8.1 0.0 copy-start.1
  8.1 1.6 %copy-done.1 = bf16[512,2048]{1,0:T(8,128)(2,1)S(1)} copy-done((bf16[512,2048]{1,0:T(8,128)(2,1)S(1)}, bf16[512,2048]{1,0:T(8,128)(2,1)}, u32[]{:S(2)}) %copy-start.1) | copy-done | bytes 2097176
  9.7 0.0 copy-start.2
  9.7 1.0 %copy-done.2 = bf16[320,576]{1,0:T(8,128)(2,1)S(1)} copy-done((bf16[320,576]{1,0:T(8,128)(2,1)S(1)}, bf16[320,576]{1,0:T(8,128)(2,1)}, u32[]{:S(2)}) %copy-start.2) | copy-done | bytes 368664
  10.7 0.0 copy-start.4
  10.7 5.1 %own_keys.1.okv_ref = bf16[16,320,256]{2,1,0:T(8,128)(2,1)} custom-call(bf16[320,576]{1,0:T(8,128)(2,1)S(1)} %copy-done.2, bf16[512,2048]{1,0:T(8,128)(2,1)S(1)} %copy-done, bf16[512,2048]{1,0:T(8,128)(2,1)S(1)} %copy-done.1), custom_call_target="tpu_custom_call" | custom-call | flops 1400000000 | bytes 8000000 | tf_op jit(solution)/shard_map/own_keys/pallas_call | solution.py:210
  15.8 0.0 copy-start.3
  15.8 2.3 %collective-permute-done.1.far = bf16[320,576]{1,0:T(8,128)(2,1)S(1)} collective-permute-done((bf16[320,576]{1,0:T(8,128)(2,1)}, bf16[320,576]{1,0:T(8,128)(2,1)S(1)}, u32[]{:S(2)}, u32[]{:S(2)}) %collective-permute-start.1) | collective-permute-done | bytes 368672 | tf_op jit(solution)/shard_map/ppermute | solution.py:275
  18.1 0.0 collective-permute-done.near
  18.1 0.0 copy-done.4
  18.1 30.0 %attend_main.1 = (bf16[320,2048]{1,0:T(8,128)(2,1)}, bf16[16,320,960]{2,1,0:T(8,128)(2,1)}, bf16[16,320,320]{2,1,0:T(8,128)(2,1)}, bf16[16,960,128]{2,1,0:T(8,12...) custom-call(s32[6]{0:T(128)S(1)} %pad_add_fusion.spans, ...), custom_call_target="tpu_custom_call" | custom-call | flops 17999998976 | bytes 35000000 | tf_op jit(solution)/shard_map/attend_main/pallas_call | solution.py:225
  48.0 5.6 %collective-permute-start.2 = (bf16[320,576]{1,0:T(8,128)(2,1)S(1)}, bf16[320,576]{1,0:T(8,128)(2,1)S(1)}, u32[]{:S(2)}, u32[]{:S(2)}) collective-permute-start(bf16[320,576]{1,0:T(8,128)(2,1)S(1)} %get-tuple-element.19), channel_id=1, source_target_pairs={{1,0},{2,1},{3,2},{4,3},{5,4},{6,5},{7,6},{8,7},{9,8},{10,9},{11,1... | collective-permute-start | bytes 1105928 | tf_op jit(solution)/shard_map/ppermute | solution.py:275
  53.7 1.5 %collective-permute-start.3 = (bf16[320,576]{1,0:T(8,128)(2,1)S(1)}, bf16[320,576]{1,0:T(8,128)(2,1)S(1)}, u32[]{:S(2)}, u32[]{:S(2)}) collective-permute-start(bf16[320,576]{1,0:T(8,128)(2,1)S(1)} %get-tuple-element.20), channel_id=1, source_target_pairs={{2,0},{3,1},{4,2},{5,3},{6,4},{7,5},{8,6},{9,7},{10,8},{11,9},{12,... | collective-permute-start | bytes 1105928 | tf_op jit(solution)/shard_map/ppermute | solution.py:275
  55.1 0.0 copy-done.3
  55.1 14.5 %attend_tail.1 = (bf16[320,3072]{1,0:T(8,128)(2,1)}, f32[320,576]{1,0:T(8,128)S(1)}) custom-call(bf16[320,3072]{1,0:T(8,128)(2,1)S(1)} %copy-done.3, bf16[320,2048]{1,0:T(8,128)(2,1)S(1)} %get-tuple-element.13.dos_ref, bf16[320,576]{1,0:T(8,128)(2,1)S(1)} %copy-done.2, bf16[320,576]{1,0:T(8,128)(2,1)S(1)} %collective-permute-done.near, ...), custom_call_target="tpu_custom_call" | custom-call | flops 8000000000 | bytes 30000000 | tf_op jit(solution)/shard_map/attend_tail/pallas_call | solution.py:258
  69.7 0.0 collective-permute-done.2
  69.7 0.0 collective-permute-done.3
  69.7 0.9 %add_convert_fusion = bf16[320,576]{1,0:T(8,128)(2,1)} fusion(bf16[320,576]{1,0:T(8,128)(2,1)S(1)} %collective-permute-done.3, f32[320,576]{1,0:T(8,128)S(1)} %get-tuple-element.18, bf16[320,576]{1,0:T(8,128)(2,1)S(1)} %collective-permute-done.2), kind=kLoop, calls=%fused_computation | loop fusion | flops 921600 | bytes 1843200 | tf_op jit(solution)/shard_map/convert_element_type | solution.py:293
  (1 shorter events, 0.0 us)
Async XLA Ops:
  0.6 17.4 %collective-permute-start.1 = (bf16[320,576]{1,0:T(8,128)(2,1)}, bf16[320,576]{1,0:T(8,128)(2,1)S(1)}, u32[]{:S(2)}, u32[]{:S(2)}) collective-permute-start(bf16[320,576]{1,0:T(8,128)(2,1)} %own.5), channel_id=1, source_target_pairs={{62,0},{63,1},{0,2},{1,3},{2,4},{3,5},{4,6},{5,7},{6,8},{7,9},{8,1... | collective-permute-start | bytes 1105928 | tf_op jit(solution)/shard_map/ppermute | solution.py:275
  3.2 14.9 %collective-permute-start = (bf16[320,576]{1,0:T(8,128)(2,1)}, bf16[320,576]{1,0:T(8,128)(2,1)S(1)}, u32[]{:S(2)}, u32[]{:S(2)}) collective-permute-start(bf16[320,576]{1,0:T(8,128)(2,1)} %own.5), channel_id=1, source_target_pairs={{63,0},{0,1},{1,2},{2,3},{3,4},{4,5},{5,6},{6,7},{7,8},{8,9},{9,10... | collective-permute-start | bytes 1105928 | tf_op jit(solution)/shard_map/ppermute | solution.py:275
  6.5 1.6 %copy-start = (bf16[512,2048]{1,0:T(8,128)(2,1)S(1)}, bf16[512,2048]{1,0:T(8,128)(2,1)}, u32[]{:S(2)}) copy-start(bf16[512,2048]{1,0:T(8,128)(2,1)} %wk_ref.5) | copy-start | bytes 6291460
  8.1 1.6 %copy-start.1 = (bf16[512,2048]{1,0:T(8,128)(2,1)S(1)}, bf16[512,2048]{1,0:T(8,128)(2,1)}, u32[]{:S(2)}) copy-start(bf16[512,2048]{1,0:T(8,128)(2,1)} %wv_ref.5) | copy-start | bytes 6291460
  9.7 1.0 %copy-start.2 = (bf16[320,576]{1,0:T(8,128)(2,1)S(1)}, bf16[320,576]{1,0:T(8,128)(2,1)}, u32[]{:S(2)}) copy-start(bf16[320,576]{1,0:T(8,128)(2,1)} %own.5) | copy-start | bytes 1105924
  10.7 7.3 %copy-start.4 = (bf16[320,2048]{1,0:T(8,128)(2,1)S(1)}, bf16[320,2048]{1,0:T(8,128)(2,1)}, u32[]{:S(2)}) copy-start(bf16[320,2048]{1,0:T(8,128)(2,1)} %do_ref.1) | copy-start | bytes 3932164
  15.8 39.3 %copy-start.3 = (bf16[320,3072]{1,0:T(8,128)(2,1)S(1)}, bf16[320,3072]{1,0:T(8,128)(2,1)}, u32[]{:S(2)}) copy-start(bf16[320,3072]{1,0:T(8,128)(2,1)} %q_ref.3) | copy-start | bytes 5898244
  48.0 21.6 %collective-permute-start.2 = (bf16[320,576]{1,0:T(8,128)(2,1)S(1)}, bf16[320,576]{1,0:T(8,128)(2,1)S(1)}, u32[]{:S(2)}, u32[]{:S(2)}) collective-permute-start(bf16[320,576]{1,0:T(8,128)(2,1)S(1)} %get-tuple-element.19), channel_id=1, source_target_pairs={{1,0},{2,1},{3,2},{4,3},{5,4},{6,5},{7,6},{8,7},{9,8},{10,9},{11,1... | collective-permute-start | bytes 1105928 | tf_op jit(solution)/shard_map/ppermute | solution.py:275
  53.7 16.0 %collective-permute-start.3 = (bf16[320,576]{1,0:T(8,128)(2,1)S(1)}, bf16[320,576]{1,0:T(8,128)(2,1)S(1)}, u32[]{:S(2)}, u32[]{:S(2)}) collective-permute-start(bf16[320,576]{1,0:T(8,128)(2,1)S(1)} %get-tuple-element.20), channel_id=1, source_target_pairs={{2,0},{3,1},{4,2},{5,3},{6,4},{7,5},{8,6},{9,7},{10,8},{11,9},{12,... | collective-permute-start | bytes 1105928 | tf_op jit(solution)/shard_map/ppermute | solution.py:275

commit v2 on v1

--- a/solution.py
+++ b/solution.py
@@ -59,13 +59,13 @@
     return base + col
 
 
-def own_keys(own, wk_ref, wv_ref, kv_ref):
+def keys_body(own, wk_ref, wv_ref, kv_ref):
     for h in range(2):
         kv_ref[h] = dot_rows(own[:, :LATENT], head_weights(wk_ref, wv_ref, h)).astype(BF)
 
 
-def main_body(spans, q_ref, do_ref, own, near, far, wk_ref, wv_ref, okv_ref,
-              out_ref, ds_ref, oe_ref, k_ref, dos_ref, tn_ref, tf_ref, bias, acc_t, rope_t):
+def main_body(spans, q_ref, do_ref, own, near, far_a, far_b, wk_ref, wv_ref, okv_ref, nkv_ref,
+              out_ref, ds_ref, oe_ref, fk_ref, dos_ref, tn_ref, tf_ref, bias, acc_t, rope_t, far, rope):
     p = pl.program_id(0)
     rows = q_ref.shape[0]
     half = rows // 2
@@ -77,22 +77,21 @@
     def _():
         row = lax.broadcasted_iota(jnp.int32, (rows, 1), 0)
         q_pos = jnp.where(row < half, pair[0] * half, (pair[1] - 1) * half) + row
+        far[...] = far_a[...] + far_b[...]
+        rope[:rows] = near[:, LATENT:]
+        rope[rows:width] = far[:, LATENT:]
+        rope[width:] = own[:, LATENT:]
         bias[...] = jnp.where(positions(rows, pair) <= q_pos, 0.0, MASKED).astype(F32)
         acc_t[...] = jnp.zeros_like(acc_t)
         rope_t[...] = jnp.zeros_like(rope_t)
 
     other_pos = positions(rows, others)
     other_bias = [jnp.where(other_pos < pair[j] * half, 0.0, MASKED).astype(F32) for j in range(2)]
-    rope = jnp.concatenate([near[:, LATENT:], far[:, LATENT:], own[:, LATENT:]], 0)
-
     def project(h):
-        w = head_weights(wk_ref, wv_ref, h)
-        kv = jnp.concatenate(
-            [dot(near[:, :LATENT], w).astype(BF), dot(far[:, :LATENT], w).astype(BF), okv_ref[h]], 0
-        )
-        k = kv[:, :NOPE]
-        k_ref[h] = k
-        return jnp.concatenate([k, rope], 1), kv[:, NOPE:]
+        fkv = dot_rows(far[:, :LATENT], head_weights(wk_ref, wv_ref, h)).astype(BF)
+        fk_ref[h] = fkv[:, :NOPE]
+        kv = jnp.concatenate([nkv_ref[h], fkv, okv_ref[h]], 0)
+        return jnp.concatenate([kv[:, :NOPE], rope[...]], 1), kv[:, NOPE:]
 
     def score(h, k):
         return dot_nt(q_head(q_ref, h), k)
@@ -120,25 +119,27 @@
         return ds
 
     k0, v0 = project(0)
+    k1, v1 = project(1)
     s0 = score(0, k0)
-    k1, v1 = project(1)
+    s1 = score(1, k1)
     e0 = soften(s0)
-    s1 = score(1, k1)
     dos0, delta0 = attend(0, e0, v0)
     e1 = soften(s1)
     dp0 = dot_nt(dos0, v0)
     dos1, delta1 = attend(1, e1, v1)
     ds0 = dscores(0, e0, dp0, delta0)
     dp1 = dot_nt(dos1, v1)
-    dv0 = dot_tn(dos0, e0[:, :width])
+    dv0 = dot_tn(dos0, e0[:, :width]).astype(BF)
     dk0 = dot_tn(q_head(q_ref, 0), ds0[:, :width]) * SCALE
+    rope_t[...] += dk0[NOPE:]
+    dk0 = dk0[:NOPE].astype(BF)
     ds1 = dscores(1, e1, dp1, delta1)
-    dv1 = dot_tn(dos1, e1[:, :width])
+    dv1 = dot_tn(dos1, e1[:, :width]).astype(BF)
     dk1 = dot_tn(q_head(q_ref, 1), ds1[:, :width]) * SCALE
-    rope_t[...] += dk0[NOPE:] + dk1[NOPE:]
-    w = jnp.concatenate([wk_ref[...], wv_ref[...]], 1)
-    d = jnp.concatenate([dk0[:NOPE].astype(BF), dk1[:NOPE].astype(BF), dv0.astype(BF), dv1.astype(BF)], 0)
-    acc_t[...] += dot(w, d)
+    rope_t[...] += dk1[NOPE:]
+    dk1 = dk1[:NOPE].astype(BF)
+    w = jnp.concatenate([wk_ref[:, 0*128:1*128+128], wv_ref[:, 0*128:1*128+128]], 1)
+    acc_t[...] += dot(w, jnp.concatenate([dk0, dk1, dv0, dv1], 0))
 
     @pl.when(p == pl.num_programs(0) - 1)
     def _():
@@ -148,24 +149,26 @@
         tf_ref[:, LATENT:] = rope_t[:, rows:].astype(BF).T
 
 
-def tail_body(q_ref, dos_ref, own, near, far, wk_ref, wv_ref, ds_ref, oe_ref, k_ref,
-              dq_ref, t_ref, acc_t, rope_t):
+def tail_body(q_ref, dos_ref, own, near, far_a, far_b, wk_ref, wv_ref, ds_ref, oe_ref, nk_ref, fk_ref, ok_ref,
+              dq_ref, t_ref, acc_t, rope_t, rope):
     p = pl.program_id(0)
     rows = q_ref.shape[0]
     width = 2 * rows
 
     @pl.when(p == 0)
     def _():
+        rope[:rows] = near[:, LATENT:]
+        rope[rows:width] = far_a[:, LATENT:] + far_b[:, LATENT:]
+        rope[width:] = own[:, LATENT:]
         acc_t[...] = jnp.zeros_like(acc_t)
         rope_t[...] = jnp.zeros_like(rope_t)
 
-    rope = jnp.concatenate([near[:, LATENT:], far[:, LATENT:], own[:, LATENT:]], 0)
     dqs, dks, dvs, rope_sum = [], [], [], None
     for h in range(2):
         ds = ds_ref[h]
         dv = dot_tn(v_head(dos_ref, h), oe_ref[h])
         dk = dot_tn(q_head(q_ref, h), ds[:, width:]) * SCALE
-        dq = dot_rows(ds, jnp.concatenate([k_ref[h], rope], 1)) * SCALE
+        dq = dot_rows(ds, jnp.concatenate([jnp.concatenate([nk_ref[h], fk_ref[h], ok_ref[h]], 0), rope[...]], 1)) * SCALE
         dqs.append(dq.astype(BF))
         dks.append(dk[:NOPE].astype(BF))
         dvs.append(dv.astype(BF))
@@ -205,21 +208,25 @@
     return jax.ShapeDtypeStruct(dims, dtype)
 
 
-def call_own_keys(own, wk, wv):
+def call_keys(own, wk, wv):
     rows = own.shape[0]
     return pl.pallas_call(
-        own_keys,
+        keys_body,
         grid=(HEADS // 2,),
         in_specs=[whole(own), columns(LATENT, 256), columns(LATENT, 256)],
         out_specs=pairs(rows, 256),
         out_shape=shape(HEADS, rows, 256),
         compiler_params=params(),
         cost_estimate=cost(7 * 10**8, 8 * 10**6),
-        name="own_keys",
+        name="project_keys",
     )(own, wk, wv)
 
 
-def call_main(spans, q, do, own, near, far, wk, wv, okv):
+def heads_block(n, rows, cols):
+    return pl.BlockSpec((n, rows, cols), lambda p, *_: (p, 0, 0))
+
+
+def call_main(spans, q, do, own, near, far_a, far_b, wk, wv, okv, nkv):
     rows = q.shape[0]
     keys = 3 * rows
     return pl.pallas_call(
@@ -227,68 +234,80 @@
         grid_spec=pltpu.PrefetchScalarGridSpec(
             num_scalar_prefetch=1,
             grid=(HEADS // 2,),
-            in_specs=[columns(rows, 2 * DQ), columns(rows, 2 * VDIM), whole(own), whole(near), whole(far),
-                      columns(LATENT, 256), columns(LATENT, 256), pairs(rows, 256)],
-            out_specs=[columns(rows, 2 * VDIM), pairs(rows, keys), pairs(rows, rows), pairs(keys, NOPE),
-                       columns(rows, 2 * VDIM), whole(near), whole(far)],
+            in_specs=[columns(rows, 2 * DQ), columns(rows, 2 * VDIM), whole(own), whole(near), whole(near), whole(near),
+                      columns(LATENT, 2 * 128), columns(LATENT, 2 * 128), heads_block(2, rows, 256), heads_block(2, rows, 256)],
+            out_specs=[columns(rows, 2 * VDIM), heads_block(2, rows, keys), heads_block(2, rows, rows), heads_block(2, rows, NOPE),
+                       columns(rows, 2 * VDIM), whole(near), whole(near)],
             scratch_shapes=[
                 pltpu.VMEM((rows, rows), F32),
                 pltpu.VMEM((LATENT, 2 * rows), F32),
                 pltpu.VMEM((ROPE, 2 * rows), F32),
+                pltpu.VMEM(near.shape, BF),
+                pltpu.VMEM((keys, ROPE), BF),
             ],
         ),
         out_shape=[
             shape(*do.shape),
             shape(HEADS, rows, keys),
             shape(HEADS, rows, rows),
-            shape(HEADS, keys, NOPE),
+            shape(HEADS, rows, NOPE),
             shape(*do.shape),
             shape(*near.shape),
-            shape(*far.shape),
+            shape(*near.shape),
         ],
         compiler_params=params(),
         cost_estimate=cost(9 * 10**9, 35 * 10**6),
         name="attend_main",
-    )(spans, q, do, own, near, far, wk, wv, okv)
-
-
-def call_tail(q, dos, own, near, far, wk, wv, ds, oe, k):
+    )(spans, q, do, own, near, far_a, far_b, wk, wv, okv, nkv)
+
+
+def call_tail(q, dos, own, near, far_a, far_b, wk, wv, ds, oe, nkv, fk, okv):
     rows = q.shape[0]
     keys = 3 * rows
     return pl.pallas_call(
         tail_body,
         grid=(HEADS // 2,),
-        in_specs=[columns(rows, 2 * DQ), columns(rows, 2 * VDIM), whole(own), whole(near), whole(far),
+        in_specs=[columns(rows, 2 * DQ), columns(rows, 2 * VDIM), whole(own), whole(near), whole(near), whole(near),
                   columns(LATENT, 256), columns(LATENT, 256),
-                  pairs(rows, keys), pairs(rows, rows), pairs(keys, NOPE)],
+                  pairs(rows, keys), pairs(rows, rows), pairs(rows, NOPE), pairs(rows, NOPE), pairs(rows, NOPE)],
         out_specs=[columns(rows, 2 * DQ), whole(own)],
-        scratch_shapes=[pltpu.VMEM((LATENT, rows), F32), pltpu.VMEM((ROPE, rows), F32)],
+        scratch_shapes=[pltpu.VMEM((LATENT, rows), F32), pltpu.VMEM((ROPE, rows), F32), pltpu.VMEM((keys, ROPE), BF)],
         out_shape=[shape(*q.shape), shape(*own.shape, dtype=F32)],
         compiler_params=params(),
         cost_estimate=cost(4 * 10**9, 30 * 10**6),
         name="attend_tail",
-    )(q, dos, own, near, far, wk, wv, ds, oe, k)
-
-
-def shifted(block, distance):
+    )(q, dos, own, near, far_a, far_b, wk, wv, ds, oe, nkv, fk, okv)
+
+
+def routed(block, distance, step=1):
     n = lax.axis_size("ctx")
-    return lax.ppermute(block, "ctx", [((i - distance) % n, i) for i in range(n)])
+    return lax.ppermute(block, "ctx", [((i - distance) % n, i) for i in range(0, n, step)])
+
+
+def to_other_core(block):
+    n = lax.axis_size("ctx")
+    return lax.ppermute(block, "ctx", [(i, i + 1) for i in range(0, n, 2)])
 
 
 def on_device(queries, latent, w_key_up, w_value_up, grad_out, span_order):
     n = lax.axis_size("ctx")
     me = lax.axis_index("ctx")
-    near = shifted(latent, 1)
-    far = shifted(latent, 2)
+    near = routed(latent, 1)
+    far_a = routed(latent, 2, 2)
+    okv = call_keys(latent, w_key_up, w_value_up)
+    near, okv = lax.optimization_barrier((near, okv))
+    far_b = to_other_core(near)
     order = span_order.reshape(n, 2)
     spans = jnp.concatenate([order[(me - lag) % n] for lag in range(3)])
-    okv = call_own_keys(latent, w_key_up, w_value_up)
-    out, ds, oe, k, dos, t_near, t_far = call_main(
-        spans, queries, grad_out, latent, near, far, w_key_up, w_value_up, okv
+    nkv = call_keys(near, w_key_up, w_value_up)
+    out, ds, oe, fk, dos, t_near, t_far = call_main(
+        spans, queries, grad_out, latent, near, far_a, far_b, w_key_up, w_value_up, okv, nkv
     )
-    from_far = shifted(t_far, -2)
-    from_near = shifted(t_near, -1)
-    dq, own_term = call_tail(queries, dos, latent, near, far, w_key_up, w_value_up, ds, oe, k)
+    from_far = routed(t_far, -2)
+    from_near = routed(t_near, -1)
+    dq, own_term = call_tail(
+        queries, dos, latent, near, far_a, far_b, w_key_up, w_value_up, ds, oe, nkv, fk, okv
+    )
     total = own_term + from_near.astype(F32) + from_far.astype(F32)
     return out, dq, total.astype(BF)
 

time: 71 us -> 72.5 us (1.021)
  the two profiles are of different devices: /device:TPU:1 before, /device:TPU:0 now
where the time goes in v2:
time: 72.5 us; the launch traced here: 71.3 us
  Pallas kernels  52.3 us (72%)
  starting transfers between devices  10.1 us (14%)
  local copies, waits for them, and re-layouts  5.92 us (8%)
  waiting for transfers between devices  1.16 us (2%)
  other arithmetic  0.98 us (1%)
  between operations  0.77 us (1%)
    pallas_call x1, Pallas kernels, call_main(): pl.pallas_call(main_body, grid_spec=pltpu.PrefetchScalarGridSpec(num_scal...  27.5 us
    pallas_call x1, Pallas kernels, call_tail(): pl.pallas_call(tail_body, grid=(HEADS // 2,), in_specs=[columns(rows, 2 *...  14.7 us
    pallas_call x2, Pallas kernels, call_keys(): pl.pallas_call(keys_body, grid=(HEADS // 2,), in_specs=[whole(own), colum...  10.1 us
    ppermute x4, starting transfers between devices, routed(): lax.ppermute(block, 'ctx', [((i - distance) % n, i) for i in range(0, n,...  8.81 us
    unnamed x14, local copies, waits for them, and re-layouts  5.78 us
  transfers between devices with their start and end apart: 5, of which 1 were waited for; matrix products, arithmetic and copies ran while one was open for 0% of the time, Pallas kernels for 35%

profile of v2, /device:TPU:0, one launch (start us, length us, event | category | flops | bytes accessed | tf_op | source)
XLA Modules:
  0.0 71.3 jit_solution(8945722134073836729)
XLA Ops:
  0.6 0.1 collective-permute-start
  0.7 3.9 %collective-permute-start.1 = (bf16[320,576]{1,0:T(8,128)(2,1)}, bf16[320,576]{1,0:T(8,128)(2,1)S(1)}, u32[]{:S(2)}, u32[]{:S(2)}) collective-permute-start(bf16[320,576]{1,0:T(8,128)(2,1)} %own.5), channel_id=1, source_target_pairs={{62,0},{0,2},{2,4},{4,6},{6,8},{8,10},{10,12},{12,14},{14,16},{16,... | collective-permute-start | bytes 1105928 | tf_op jit(solution)/shard_map/ppermute | solution.py:284
  4.6 0.0 copy-start
  4.6 1.6 %copy-done = bf16[512,2048]{1,0:T(8,128)(2,1)S(1)} copy-done((bf16[512,2048]{1,0:T(8,128)(2,1)S(1)}, bf16[512,2048]{1,0:T(8,128)(2,1)}, u32[]{:S(2)}) %copy-start) | copy-done | bytes 2097176
  6.2 1.6 %copy-done.2 = bf16[512,2048]{1,0:T(8,128)(2,1)S(1)} copy-done((bf16[512,2048]{1,0:T(8,128)(2,1)S(1)}, bf16[512,2048]{1,0:T(8,128)(2,1)}, u32[]{:S(2)}) %copy-start.2) | copy-done | bytes 2097176
  7.8 1.0 %copy-done.4 = bf16[320,576]{1,0:T(8,128)(2,1)S(1)} copy-done((bf16[320,576]{1,0:T(8,128)(2,1)S(1)}, bf16[320,576]{1,0:T(8,128)(2,1)}, u32[]{:S(2)}) %copy-start.4) | copy-done | bytes 368664
  8.8 5.1 %project_keys.2.okv_ref.ok_ref = bf16[16,320,256]{2,1,0:T(8,128)(2,1)} custom-call(bf16[320,576]{1,0:T(8,128)(2,1)S(1)} %copy-done.4, bf16[512,2048]{1,0:T(8,128)(2,1)S(1)} %copy-done, bf16[512,2048]{1,0:T(8,128)(2,1)S(1)} %copy-done.2), custom_call_target="tpu_custom_call" | custom-call | flops 1400000000 | bytes 8000000 | tf_op jit(solution)/shard_map/project_keys/pallas_call | solution.py:213
  13.9 1.2 %collective-permute-done.own.near = bf16[320,576]{1,0:T(8,128)(2,1)S(1)} collective-permute-done((bf16[320,576]{1,0:T(8,128)(2,1)}, bf16[320,576]{1,0:T(8,128)(2,1)S(1)}, u32[]{:S(2)}, u32[]{:S(2)}) %collective-permute-start) | collective-permute-done | bytes 368672 | tf_op jit(solution)/shard_map/ppermute | solution.py:284
  15.0 1.3 %collective-permute-start.2 = (bf16[320,576]{1,0:T(8,128)(2,1)S(1)}, bf16[320,576]{1,0:T(8,128)(2,1)S(1)}, u32[]{:S(2)}, u32[]{:S(2)}) collective-permute-start(bf16[320,576]{1,0:T(8,128)(2,1)S(1)} %collective-permute-done.own.near), channel_id=1, source_target_pairs={{0,1},{2,3},{4,5},{6,7},{8,9},{10,11},{12,13},{14,15},{16,17},{18,... | collective-permute-start | bytes 1105928 | tf_op jit(solution)/shard_map/ppermute | solution.py:289
  16.4 0.0 copy-done.6
  16.4 0.1 reshape.9
  16.6 0.1 pad_add_fusion.spans
  16.7 1.6 %copy-done.3 = bf16[512,2048]{1,0:T(8,128)(2,1)S(1)} copy-done((bf16[512,2048]{1,0:T(8,128)(2,1)S(1)}, bf16[512,2048]{1,0:T(8,128)(2,1)}, u32[]{:S(2)}) %copy-start.3) | copy-done | bytes 2097176
  18.3 5.1 %project_keys.3.nkv_ref.nk_ref = bf16[16,320,256]{2,1,0:T(8,128)(2,1)} custom-call(bf16[320,576]{1,0:T(8,128)(2,1)S(1)} %collective-permute-done.own.near, bf16[512,2048]{1,0:T(8,128)(2,1)S(1)} %copy-done.1, bf16[512,2048]{1,0:T(8,128)(2,1)S(1)} %copy-done.3), custom_call_target="tpu_custom_call" | custom-call | flops 1400000000 | bytes 8000000 | tf_op jit(solution)/shard_map/project_keys/pallas_call | solution.py:213
  23.3 0.0 collective-permute-done.1.far_a
  23.3 0.0 collective-permute-done.2.far_b
  23.3 0.0 copy-done.5
  23.3 27.5 %attend_main.1 = (bf16[320,2048]{1,0:T(8,128)(2,1)}, bf16[16,320,960]{2,1,0:T(8,128)(2,1)}, bf16[16,320,320]{2,1,0:T(8,128)(2,1)}, bf16[16,320,128]{2,1,0:T(8,12...) custom-call(s32[6]{0:T(128)S(1)} %pad_add_fusion.spans, ...), custom_call_target="tpu_custom_call" | custom-call | flops 17999998976 | bytes 35000000 | tf_op jit(solution)/shard_map/attend_main/pallas_call | solution.py:232
  50.9 2.5 %collective-permute-start.3 = (bf16[320,576]{1,0:T(8,128)(2,1)S(1)}, bf16[320,576]{1,0:T(8,128)(2,1)S(1)}, u32[]{:S(2)}, u32[]{:S(2)}) collective-permute-start(bf16[320,576]{1,0:T(8,128)(2,1)S(1)} %get-tuple-element.23), channel_id=1, source_target_pairs={{1,0},{2,1},{3,2},{4,3},{5,4},{6,5},{7,6},{8,7},{9,8},{10,9},{11,1... | collective-permute-start | bytes 1105928 | tf_op jit(solution)/shard_map/ppermute | solution.py:284
  53.4 2.3 %collective-permute-start.4 = (bf16[320,576]{1,0:T(8,128)(2,1)S(1)}, bf16[320,576]{1,0:T(8,128)(2,1)S(1)}, u32[]{:S(2)}, u32[]{:S(2)}) collective-permute-start(bf16[320,576]{1,0:T(8,128)(2,1)S(1)} %get-tuple-element.24), channel_id=1, source_target_pairs={{2,0},{3,1},{4,2},{5,3},{6,4},{7,5},{8,6},{9,7},{10,8},{11,9},{12,... | collective-permute-start | bytes 1105928 | tf_op jit(solution)/shard_map/ppermute | solution.py:284
  55.7 14.7 %attend_tail.1 = (bf16[320,3072]{1,0:T(8,128)(2,1)}, f32[320,576]{1,0:T(8,128)S(1)}) custom-call(bf16[320,3072]{1,0:T(8,128)(2,1)} %q_ref.3, bf16[320,2048]{1,0:T(8,128)(2,1)S(1)} %get-tuple-element.17.dos_ref, bf16[320,576]{1,0:T(8,128)(2,1)S(1)} %copy-done.5, bf16[320,576]{1,0:T(8,128)(2,1)S(1)} %collective-permute-done.own.near, ...), custom_call_target="tpu_custom_call" | custom-call | flops 8000000000 | bytes 30000000 | tf_op jit(solution)/shard_map/attend_tail/pallas_call | solution.py:267
  70.4 0.0 collective-permute-done.3
  70.4 0.0 collective-permute-done.4
  70.4 0.9 %add_convert_fusion = bf16[320,576]{1,0:T(8,128)(2,1)} fusion(bf16[320,576]{1,0:T(8,128)(2,1)S(1)} %collective-permute-done.4, f32[320,576]{1,0:T(8,128)S(1)} %get-tuple-element.22, bf16[320,576]{1,0:T(8,128)(2,1)S(1)} %collective-permute-done.3), kind=kLoop, calls=%fused_computation | loop fusion | flops 921600 | bytes 1843200 | tf_op jit(solution)/shard_map/convert_element_type | solution.py:312
  (8 shorter events, 0.0 us)
Async XLA Ops:
  0.6 14.4 %collective-permute-start = (bf16[320,576]{1,0:T(8,128)(2,1)}, bf16[320,576]{1,0:T(8,128)(2,1)S(1)}, u32[]{:S(2)}, u32[]{:S(2)}) collective-permute-start(bf16[320,576]{1,0:T(8,128)(2,1)} %own.5), channel_id=1, source_target_pairs={{63,0},{0,1},{1,2},{2,3},{3,4},{4,5},{5,6},{6,7},{7,8},{8,9},{9,10... | collective-permute-start | bytes 1105928 | tf_op jit(solution)/shard_map/ppermute | solution.py:284
  0.7 22.6 %collective-permute-start.1 = (bf16[320,576]{1,0:T(8,128)(2,1)}, bf16[320,576]{1,0:T(8,128)(2,1)S(1)}, u32[]{:S(2)}, u32[]{:S(2)}) collective-permute-start(bf16[320,576]{1,0:T(8,128)(2,1)} %own.5), channel_id=1, source_target_pairs={{62,0},{0,2},{2,4},{4,6},{6,8},{8,10},{10,12},{12,14},{14,16},{16,... | collective-permute-start | bytes 1105928 | tf_op jit(solution)/shard_map/ppermute | solution.py:284
  4.6 1.6 %copy-start = (bf16[512,2048]{1,0:T(8,128)(2,1)S(1)}, bf16[512,2048]{1,0:T(8,128)(2,1)}, u32[]{:S(2)}) copy-start(bf16[512,2048]{1,0:T(8,128)(2,1)} %wk_ref.7) | copy-start | bytes 6291460
  6.2 1.6 %copy-start.2 = (bf16[512,2048]{1,0:T(8,128)(2,1)S(1)}, bf16[512,2048]{1,0:T(8,128)(2,1)}, u32[]{:S(2)}) copy-start(bf16[512,2048]{1,0:T(8,128)(2,1)} %wv_ref.7) | copy-start | bytes 6291460
  7.8 1.0 %copy-start.4 = (bf16[320,576]{1,0:T(8,128)(2,1)S(1)}, bf16[320,576]{1,0:T(8,128)(2,1)}, u32[]{:S(2)}) copy-start(bf16[320,576]{1,0:T(8,128)(2,1)} %own.5) | copy-start | bytes 1105924
  8.8 7.6 %copy-start.6 = (s32[128]{0:T(128)S(1)}, s32[128]{0:T(128)}, u32[]{:S(2)}) copy-start(s32[128]{0:T(128)} %param.11) | copy-start | bytes 1540
  8.8 7.8 %copy-start.1 = (bf16[512,2048]{1,0:T(8,128)(2,1)S(1)}, bf16[512,2048]{1,0:T(8,128)(2,1)}, u32[]{:S(2)}) copy-start(bf16[512,2048]{1,0:T(8,128)(2,1)} %wk_ref.7) | copy-start | bytes 6291460
  15.0 8.3 %collective-permute-start.2 = (bf16[320,576]{1,0:T(8,128)(2,1)S(1)}, bf16[320,576]{1,0:T(8,128)(2,1)S(1)}, u32[]{:S(2)}, u32[]{:S(2)}) collective-permute-start(bf16[320,576]{1,0:T(8,128)(2,1)S(1)} %collective-permute-done.own.near), channel_id=1, source_target_pairs={{0,1},{2,3},{4,5},{6,7},{8,9},{10,11},{12,13},{14,15},{16,17},{18,... | collective-permute-start | bytes 1105928 | tf_op jit(solution)/shard_map/ppermute | solution.py:289
  16.7 1.6 %copy-start.3 = (bf16[512,2048]{1,0:T(8,128)(2,1)S(1)}, bf16[512,2048]{1,0:T(8,128)(2,1)}, u32[]{:S(2)}) copy-start(bf16[512,2048]{1,0:T(8,128)(2,1)} %wv_ref.7) | copy-start | bytes 6291460
  18.3 5.1 %copy-start.5 = (bf16[320,576]{1,0:T(8,128)(2,1)S(1)}, bf16[320,576]{1,0:T(8,128)(2,1)}, u32[]{:S(2)}) copy-start(bf16[320,576]{1,0:T(8,128)(2,1)} %own.5) | copy-start | bytes 1105924
  50.9 19.5 %collective-permute-start.3 = (bf16[320,576]{1,0:T(8,128)(2,1)S(1)}, bf16[320,576]{1,0:T(8,128)(2,1)S(1)}, u32[]{:S(2)}, u32[]{:S(2)}) collective-permute-start(bf16[320,576]{1,0:T(8,128)(2,1)S(1)} %get-tuple-element.23), channel_id=1, source_target_pairs={{1,0},{2,1},{3,2},{4,3},{5,4},{6,5},{7,6},{8,7},{9,8},{10,9},{11,1... | collective-permute-start | bytes 1105928 | tf_op jit(solution)/shard_map/ppermute | solution.py:284
  53.4 17.0 %collective-permute-start.4 = (bf16[320,576]{1,0:T(8,128)(2,1)S(1)}, bf16[320,576]{1,0:T(8,128)(2,1)S(1)}, u32[]{:S(2)}, u32[]{:S(2)}) collective-permute-start(bf16[320,576]{1,0:T(8,128)(2,1)S(1)} %get-tuple-element.24), channel_id=1, source_target_pairs={{2,0},{3,1},{4,2},{5,3},{6,4},{7,5},{8,6},{9,7},{10,8},{11,9},{12,... | collective-permute-start | bytes 1105928 | tf_op jit(solution)/shard_map/ppermute | solution.py:284

commit v3 on v2

--- a/solution.py
+++ b/solution.py
@@ -60,12 +60,14 @@
 
 
 def keys_body(own, wk_ref, wv_ref, kv_ref):
+    w = jnp.concatenate([head_weights(wk_ref, wv_ref, h) for h in range(2)], 1)
+    kv = dot(own[:, :LATENT], w).astype(BF)
     for h in range(2):
-        kv_ref[h] = dot_rows(own[:, :LATENT], head_weights(wk_ref, wv_ref, h)).astype(BF)
-
-
-def main_body(spans, q_ref, do_ref, own, near, far_a, far_b, wk_ref, wv_ref, okv_ref, nkv_ref,
-              out_ref, ds_ref, oe_ref, fk_ref, dos_ref, tn_ref, tf_ref, bias, acc_t, rope_t, far, rope):
+        kv_ref[h] = kv[:, h * 256 : (h + 1) * 256]
+
+
+def main_body(spans, q_ref, do_ref, own, near, far_a, far_b, wk_ref, wv_ref, okv_ref,
+              out_ref, dq_ref, ds_ref, oe_ref, dos_ref, tn_ref, tf_ref, bias, acc_t, rope_t, others_lat, rope, held_d, held_w):
     p = pl.program_id(0)
     rows = q_ref.shape[0]
     half = rows // 2
@@ -77,20 +79,22 @@
     def _():
         row = lax.broadcasted_iota(jnp.int32, (rows, 1), 0)
         q_pos = jnp.where(row < half, pair[0] * half, (pair[1] - 1) * half) + row
-        far[...] = far_a[...] + far_b[...]
+        others_lat[:rows] = near[:, :LATENT]
+        others_lat[rows:] = far_a[:, :LATENT] + far_b[:, :LATENT]
         rope[:rows] = near[:, LATENT:]
-        rope[rows:width] = far[:, LATENT:]
+        rope[rows:width] = far_a[:, LATENT:] + far_b[:, LATENT:]
         rope[width:] = own[:, LATENT:]
         bias[...] = jnp.where(positions(rows, pair) <= q_pos, 0.0, MASKED).astype(F32)
         acc_t[...] = jnp.zeros_like(acc_t)
+        held_d[...] = jnp.zeros_like(held_d)
+        held_w[...] = jnp.zeros_like(held_w)
         rope_t[...] = jnp.zeros_like(rope_t)
 
     other_pos = positions(rows, others)
     other_bias = [jnp.where(other_pos < pair[j] * half, 0.0, MASKED).astype(F32) for j in range(2)]
     def project(h):
-        fkv = dot_rows(far[:, :LATENT], head_weights(wk_ref, wv_ref, h)).astype(BF)
-        fk_ref[h] = fkv[:, :NOPE]
-        kv = jnp.concatenate([nkv_ref[h], fkv, okv_ref[h]], 0)
+        kv = dot_rows(others_lat[...], head_weights(wk_ref, wv_ref, h)).astype(BF)
+        kv = jnp.concatenate([kv, okv_ref[h]], 0)
         return jnp.concatenate([kv[:, :NOPE], rope[...]], 1), kv[:, NOPE:]
 
     def score(h, k):
@@ -115,7 +119,7 @@
 
     def dscores(h, e, dp, delta):
         ds = (e.astype(F32) * (dp - delta)).astype(BF)
-        ds_ref[h] = ds
+        ds_ref[h] = ds[:, width:]
         return ds
 
     k0, v0 = project(0)
@@ -123,8 +127,10 @@
     s0 = score(0, k0)
     s1 = score(1, k1)
     e0 = soften(s0)
+    acc_t[: LATENT // 2] += dot(held_w[: LATENT // 2], held_d[...])
     dos0, delta0 = attend(0, e0, v0)
     e1 = soften(s1)
+    acc_t[LATENT // 2 :] += dot(held_w[LATENT // 2 :], held_d[...])
     dp0 = dot_nt(dos0, v0)
     dos1, delta1 = attend(1, e1, v1)
     ds0 = dscores(0, e0, dp0, delta0)
@@ -133,50 +139,40 @@
     dk0 = dot_tn(q_head(q_ref, 0), ds0[:, :width]) * SCALE
     rope_t[...] += dk0[NOPE:]
     dk0 = dk0[:NOPE].astype(BF)
+    dq0 = (dot_rows(ds0, k0) * SCALE).astype(BF)
     ds1 = dscores(1, e1, dp1, delta1)
     dv1 = dot_tn(dos1, e1[:, :width]).astype(BF)
     dk1 = dot_tn(q_head(q_ref, 1), ds1[:, :width]) * SCALE
     rope_t[...] += dk1[NOPE:]
     dk1 = dk1[:NOPE].astype(BF)
-    w = jnp.concatenate([wk_ref[:, 0*128:1*128+128], wv_ref[:, 0*128:1*128+128]], 1)
-    acc_t[...] += dot(w, jnp.concatenate([dk0, dk1, dv0, dv1], 0))
+    dq1 = (dot_rows(ds1, k1) * SCALE).astype(BF)
+    dq_ref[:, 0*DQ:(1+1)*DQ] = jnp.concatenate([dq0, dq1], 1)
+    held_w[...] = jnp.concatenate([wk_ref[...], wv_ref[...]], 1)
+    held_d[...] = jnp.concatenate([dk0, dk1, dv0, dv1], 0)
 
     @pl.when(p == pl.num_programs(0) - 1)
     def _():
+        acc_t[...] += dot(held_w[...], held_d[...])
         tn_ref[:, :LATENT] = acc_t[:, :rows].astype(BF).T
         tn_ref[:, LATENT:] = rope_t[:, :rows].astype(BF).T
         tf_ref[:, :LATENT] = acc_t[:, rows:].astype(BF).T
         tf_ref[:, LATENT:] = rope_t[:, rows:].astype(BF).T
 
 
-def tail_body(q_ref, dos_ref, own, near, far_a, far_b, wk_ref, wv_ref, ds_ref, oe_ref, nk_ref, fk_ref, ok_ref,
-              dq_ref, t_ref, acc_t, rope_t, rope):
+def tail_body(q_ref, dos_ref, wk_ref, wv_ref, ds_ref, oe_ref, t_ref, acc_t, rope_t):
     p = pl.program_id(0)
-    rows = q_ref.shape[0]
-    width = 2 * rows
 
     @pl.when(p == 0)
     def _():
-        rope[:rows] = near[:, LATENT:]
-        rope[rows:width] = far_a[:, LATENT:] + far_b[:, LATENT:]
-        rope[width:] = own[:, LATENT:]
         acc_t[...] = jnp.zeros_like(acc_t)
         rope_t[...] = jnp.zeros_like(rope_t)
 
-    dqs, dks, dvs, rope_sum = [], [], [], None
-    for h in range(2):
-        ds = ds_ref[h]
-        dv = dot_tn(v_head(dos_ref, h), oe_ref[h])
-        dk = dot_tn(q_head(q_ref, h), ds[:, width:]) * SCALE
-        dq = dot_rows(ds, jnp.concatenate([jnp.concatenate([nk_ref[h], fk_ref[h], ok_ref[h]], 0), rope[...]], 1)) * SCALE
-        dqs.append(dq.astype(BF))
-        dks.append(dk[:NOPE].astype(BF))
-        dvs.append(dv.astype(BF))
-        rope_sum = dk[NOPE:] if rope_sum is None else rope_sum + dk[NOPE:]
-    dq_ref[...] = jnp.concatenate(dqs, 1)
-    rope_t[...] += rope_sum
+    heads = range(2)
+    dvs = [dot_tn(v_head(dos_ref, h), oe_ref[h]).astype(BF) for h in heads]
+    dks = [dot_tn(q_head(q_ref, h), ds_ref[h]) * SCALE for h in heads]
+    rope_t[...] += dks[0][NOPE:] + dks[1][NOPE:]
     w = jnp.concatenate([wk_ref[...], wv_ref[...]], 1)
-    acc_t[...] += dot(w, jnp.concatenate(dks + dvs, 0))
+    acc_t[...] += dot(w, jnp.concatenate([dk[:NOPE].astype(BF) for dk in dks] + dvs, 0))
 
     @pl.when(p == pl.num_programs(0) - 1)
     def _():
@@ -226,7 +222,7 @@
     return pl.BlockSpec((n, rows, cols), lambda p, *_: (p, 0, 0))
 
 
-def call_main(spans, q, do, own, near, far_a, far_b, wk, wv, okv, nkv):
+def call_main(spans, q, do, own, near, far_a, far_b, wk, wv, okv):
     rows = q.shape[0]
     keys = 3 * rows
     return pl.pallas_call(
@@ -235,22 +231,24 @@
             num_scalar_prefetch=1,
             grid=(HEADS // 2,),
             in_specs=[columns(rows, 2 * DQ), columns(rows, 2 * VDIM), whole(own), whole(near), whole(near), whole(near),
-                      columns(LATENT, 2 * 128), columns(LATENT, 2 * 128), heads_block(2, rows, 256), heads_block(2, rows, 256)],
-            out_specs=[columns(rows, 2 * VDIM), heads_block(2, rows, keys), heads_block(2, rows, rows), heads_block(2, rows, NOPE),
+                      columns(LATENT, 2 * 128), columns(LATENT, 2 * 128), heads_block(2, rows, 256)],
+            out_specs=[columns(rows, 2 * VDIM), columns(rows, 2 * DQ), heads_block(2, rows, rows), heads_block(2, rows, rows),
                        columns(rows, 2 * VDIM), whole(near), whole(near)],
             scratch_shapes=[
                 pltpu.VMEM((rows, rows), F32),
                 pltpu.VMEM((LATENT, 2 * rows), F32),
                 pltpu.VMEM((ROPE, 2 * rows), F32),
-                pltpu.VMEM(near.shape, BF),
+                pltpu.VMEM((2 * rows, LATENT), BF),
                 pltpu.VMEM((keys, ROPE), BF),
+                pltpu.VMEM((4 * NOPE, 2 * rows), BF),
+                pltpu.VMEM((LATENT, 4 * NOPE), BF),
             ],
         ),
         out_shape=[
             shape(*do.shape),
-            shape(HEADS, rows, keys),
+            shape(*q.shape),
             shape(HEADS, rows, rows),
-            shape(HEADS, rows, NOPE),
+            shape(HEADS, rows, rows),
             shape(*do.shape),
             shape(*near.shape),
             shape(*near.shape),
@@ -258,25 +256,23 @@
         compiler_params=params(),
         cost_estimate=cost(9 * 10**9, 35 * 10**6),
         name="attend_main",
-    )(spans, q, do, own, near, far_a, far_b, wk, wv, okv, nkv)
-
-
-def call_tail(q, dos, own, near, far_a, far_b, wk, wv, ds, oe, nkv, fk, okv):
+    )(spans, q, do, own, near, far_a, far_b, wk, wv, okv)
+
+
+def call_tail(q, dos, own, wk, wv, ds, oe):
     rows = q.shape[0]
-    keys = 3 * rows
     return pl.pallas_call(
         tail_body,
         grid=(HEADS // 2,),
-        in_specs=[columns(rows, 2 * DQ), columns(rows, 2 * VDIM), whole(own), whole(near), whole(near), whole(near),
-                  columns(LATENT, 256), columns(LATENT, 256),
-                  pairs(rows, keys), pairs(rows, rows), pairs(rows, NOPE), pairs(rows, NOPE), pairs(rows, NOPE)],
-        out_specs=[columns(rows, 2 * DQ), whole(own)],
-        scratch_shapes=[pltpu.VMEM((LATENT, rows), F32), pltpu.VMEM((ROPE, rows), F32), pltpu.VMEM((keys, ROPE), BF)],
-        out_shape=[shape(*q.shape), shape(*own.shape, dtype=F32)],
+        in_specs=[columns(rows, 2 * DQ), columns(rows, 2 * VDIM), columns(LATENT, 256), columns(LATENT, 256),
+                  pairs(rows, rows), pairs(rows, rows)],
+        out_specs=whole(own),
+        scratch_shapes=[pltpu.VMEM((LATENT, rows), F32), pltpu.VMEM((ROPE, rows), F32)],
+        out_shape=shape(*own.shape, dtype=F32),
         compiler_params=params(),
-        cost_estimate=cost(4 * 10**9, 30 * 10**6),
+        cost_estimate=cost(3 * 10**9, 16 * 10**6),
         name="attend_tail",
-    )(q, dos, own, near, far_a, far_b, wk, wv, ds, oe, nkv, fk, okv)
+    )(q, dos, wk, wv, ds, oe)
 
 
 def routed(block, distance, step=1):
@@ -299,15 +295,12 @@
     far_b = to_other_core(near)
     order = span_order.reshape(n, 2)
     spans = jnp.concatenate([order[(me - lag) % n] for lag in range(3)])
-    nkv = call_keys(near, w_key_up, w_value_up)
-    out, ds, oe, fk, dos, t_near, t_far = call_main(
-        spans, queries, grad_out, latent, near, far_a, far_b, w_key_up, w_value_up, okv, nkv
+    out, dq, ds, oe, dos, t_near, t_far = call_main(
+        spans, queries, grad_out, latent, near, far_a, far_b, w_key_up, w_value_up, okv
     )
     from_far = routed(t_far, -2)
     from_near = routed(t_near, -1)
-    dq, own_term = call_tail(
-        queries, dos, latent, near, far_a, far_b, w_key_up, w_value_up, ds, oe, nkv, fk, okv
-    )
+    own_term = call_tail(queries, dos, latent, w_key_up, w_value_up, ds, oe)
     total = own_term + from_near.astype(F32) + from_far.astype(F32)
     return out, dq, total.astype(BF)
 

time: 72.5 us -> 67 us (0.924); the launches traced: 71.3 us -> 66.5 us
  Pallas kernels: 52.3 us -> 45.6 us
  waiting for transfers between devices: 1.16 us -> 3.39 us
  local copies, waits for them, and re-layouts: 5.92 us -> 4.34 us
  starting transfers between devices: 10.1 us -> 11.5 us
    pallas_call x2 -> x1, Pallas kernels: 10.1 us -> 5.11 us  [call_keys(): pl.pallas_call(keys_body, grid=(HEADS // 2,), in_specs=[whole(own), colum...]
    pallas_call x1, Pallas kernels: 14.7 us -> 10.7 us  [call_tail(): pl.pallas_call(tail_body, grid=(HEADS // 2,), in_specs=[columns(rows, 2 *...]
    pallas_call x1, Pallas kernels: 27.5 us -> 29.8 us  [call_main(): pl.pallas_call(main_body, grid_spec=pltpu.PrefetchScalarGridSpec(num_scal...]
    ppermute x4, waiting for transfers between devices: 1.16 us -> 3.39 us  [routed(): lax.ppermute(block, 'ctx', [((i - distance) % n, i) for i in range(0, n,...]
    unnamed x14 -> x16, local copies, waits for them, and re-layouts: 5.78 us -> 4.2 us
    ppermute x4, starting transfers between devices: 8.81 us -> 10.2 us  [routed(): lax.ppermute(block, 'ctx', [((i - distance) % n, i) for i in range(0, n,...]
  transfers between devices with their start and end apart: 5 -> 5, of which waited for: 1 -> 3; matrix products, arithmetic and copies ran while one was open for 0% -> 0% of each run, Pallas kernels for 35% -> 24%
where the time goes in v3:
time: 67 us; the launch traced here: 66.5 us
  Pallas kernels  45.6 us (68%)
  starting transfers between devices  11.5 us (17%)
  local copies, waits for them, and re-layouts  4.34 us (6%)
  waiting for transfers between devices  3.39 us (5%)
  other arithmetic  0.95 us (1%)
  between operations  0.78 us (1%)
    pallas_call x1, Pallas kernels, call_main(): pl.pallas_call(main_body, grid_spec=pltpu.PrefetchScalarGridSpec(num_scal...  29.8 us
    pallas_call x1, Pallas kernels, call_tail(): pl.pallas_call(tail_body, grid=(HEADS // 2,), in_specs=[columns(rows, 2 *...  10.7 us
    ppermute x4, starting transfers between devices, routed(): lax.ppermute(block, 'ctx', [((i - distance) % n, i) for i in range(0, n,...  10.2 us
    pallas_call x1, Pallas kernels, call_keys(): pl.pallas_call(keys_body, grid=(HEADS // 2,), in_specs=[whole(own), colum...  5.11 us
    unnamed x16, local copies, waits for them, and re-layouts  4.2 us
    ppermute x4, waiting for transfers between devices, routed(): lax.ppermute(block, 'ctx', [((i - distance) % n, i) for i in range(0, n,...  3.39 us
  transfers between devices with their start and end apart: 5, of which 3 were waited for; matrix products, arithmetic and copies ran while one was open for 0% of the time, Pallas kernels for 24%

profile of v3, /device:TPU:0, one launch (start us, length us, event | category | flops | bytes accessed | tf_op | source)
XLA Modules:
  0.0 66.5 jit_solution(7971671680309850347)
XLA Ops:
  0.6 0.1 collective-permute-start
  0.7 3.9 %collective-permute-start.1 = (bf16[320,576]{1,0:T(8,128)(2,1)}, bf16[320,576]{1,0:T(8,128)(2,1)S(1)}, u32[]{:S(2)}, u32[]{:S(2)}) collective-permute-start(bf16[320,576]{1,0:T(8,128)(2,1)} %own.3), channel_id=1, source_target_pairs={{62,0},{0,2},{2,4},{4,6},{6,8},{8,10},{10,12},{12,14},{14,16},{16,... | collective-permute-start | bytes 1105928 | tf_op jit(solution)/shard_map/ppermute | solution.py:280
  4.6 0.0 copy-start
  4.6 1.6 %copy-done = bf16[512,2048]{1,0:T(8,128)(2,1)S(1)} copy-done((bf16[512,2048]{1,0:T(8,128)(2,1)S(1)}, bf16[512,2048]{1,0:T(8,128)(2,1)}, u32[]{:S(2)}) %copy-start) | copy-done | bytes 2097176
  6.2 1.6 %copy-done.2 = bf16[512,2048]{1,0:T(8,128)(2,1)S(1)} copy-done((bf16[512,2048]{1,0:T(8,128)(2,1)S(1)}, bf16[512,2048]{1,0:T(8,128)(2,1)}, u32[]{:S(2)}) %copy-start.2) | copy-done | bytes 2097176
  7.8 1.0 %copy-done.3 = bf16[320,576]{1,0:T(8,128)(2,1)S(1)} copy-done((bf16[320,576]{1,0:T(8,128)(2,1)S(1)}, bf16[320,576]{1,0:T(8,128)(2,1)}, u32[]{:S(2)}) %copy-start.3) | copy-done | bytes 368664
  8.8 5.1 %project_keys.1.okv_ref = bf16[16,320,256]{2,1,0:T(8,128)(2,1)} custom-call(bf16[320,576]{1,0:T(8,128)(2,1)S(1)} %copy-done.3, bf16[512,2048]{1,0:T(8,128)(2,1)S(1)} %copy-done, bf16[512,2048]{1,0:T(8,128)(2,1)S(1)} %copy-done.2), custom_call_target="tpu_custom_call" | custom-call | flops 1400000000 | bytes 8000000 | tf_op jit(solution)/shard_map/project_keys/pallas_call | solution.py:209
  13.9 1.1 %collective-permute-done.near = bf16[320,576]{1,0:T(8,128)(2,1)S(1)} collective-permute-done((bf16[320,576]{1,0:T(8,128)(2,1)}, bf16[320,576]{1,0:T(8,128)(2,1)S(1)}, u32[]{:S(2)}, u32[]{:S(2)}) %collective-permute-start) | collective-permute-done | bytes 368672 | tf_op jit(solution)/shard_map/ppermute | solution.py:280
  15.0 1.3 %collective-permute-start.2 = (bf16[320,576]{1,0:T(8,128)(2,1)S(1)}, bf16[320,576]{1,0:T(8,128)(2,1)S(1)}, u32[]{:S(2)}, u32[]{:S(2)}) collective-permute-start(bf16[320,576]{1,0:T(8,128)(2,1)S(1)} %collective-permute-done.near), channel_id=1, source_target_pairs={{0,1},{2,3},{4,5},{6,7},{8,9},{10,11},{12,13},{14,15},{16,17},{18,... | collective-permute-start | bytes 1105928 | tf_op jit(solution)/shard_map/ppermute | solution.py:285
  16.4 0.0 copy-done.7
  16.4 0.1 reshape.9
  16.6 0.1 pad_add_fusion.spans
  16.7 1.2 %collective-permute-done.1.far_a = bf16[320,576]{1,0:T(8,128)(2,1)S(1)} collective-permute-done((bf16[320,576]{1,0:T(8,128)(2,1)}, bf16[320,576]{1,0:T(8,128)(2,1)S(1)}, u32[]{:S(2)}, u32[]{:S(2)}) %collective-permute-start.1) | collective-permute-done | bytes 368672 | tf_op jit(solution)/shard_map/ppermute | solution.py:280
  17.9 0.0 collective-permute-done.2.far_b
  17.9 0.0 copy-done.4
  17.9 0.0 copy-done.6
  17.9 29.8 %attend_main.1 = (bf16[320,2048]{1,0:T(8,128)(2,1)}, bf16[320,3072]{1,0:T(8,128)(2,1)}, bf16[16,320,320]{2,1,0:T(8,128)(2,1)}, bf16[16,320,320]{2,1,0:T(8,128)(2...) custom-call(s32[6]{0:T(128)S(1)} %pad_add_fusion.spans, ...), custom_call_target="tpu_custom_call" | custom-call | flops 17999998976 | bytes 35000000 | tf_op jit(solution)/shard_map/attend_main/pallas_call | solution.py:228
  47.7 4.2 %collective-permute-start.3 = (bf16[320,576]{1,0:T(8,128)(2,1)S(1)}, bf16[320,576]{1,0:T(8,128)(2,1)S(1)}, u32[]{:S(2)}, u32[]{:S(2)}) collective-permute-start(bf16[320,576]{1,0:T(8,128)(2,1)S(1)} %get-tuple-element.19), channel_id=1, source_target_pairs={{1,0},{2,1},{3,2},{4,3},{5,4},{6,5},{7,6},{8,7},{9,8},{10,9},{11,1... | collective-permute-start | bytes 1105928 | tf_op jit(solution)/shard_map/ppermute | solution.py:280
  51.8 2.0 %collective-permute-start.4 = (bf16[320,576]{1,0:T(8,128)(2,1)S(1)}, bf16[320,576]{1,0:T(8,128)(2,1)S(1)}, u32[]{:S(2)}, u32[]{:S(2)}) collective-permute-start(bf16[320,576]{1,0:T(8,128)(2,1)S(1)} %get-tuple-element.20), channel_id=1, source_target_pairs={{2,0},{3,1},{4,2},{5,3},{6,4},{7,5},{8,6},{9,7},{10,8},{11,9},{12,... | collective-permute-start | bytes 1105928 | tf_op jit(solution)/shard_map/ppermute | solution.py:280
  53.9 0.0 copy-done.5
  53.9 10.7 %attend_tail.1 = f32[320,576]{1,0:T(8,128)S(1)} custom-call(bf16[320,3072]{1,0:T(8,128)(2,1)S(1)} %copy-done.5, bf16[320,2048]{1,0:T(8,128)(2,1)S(1)} %get-tuple-element.16.dos_ref, bf16[512,2048]{1,0:T(8,128)(2,1)S(1)} %copy-done.1, bf16[512,2048]{1,0:T(8,128)(2,1)} %wv_ref.5, bf16[16,320,320]{2,1,0:T(8,128)(2,1)} %get-tuple-element.17.ds_ref, ...), custom_call_target="tpu_custom_call" | custom-call | flops 6000000000 | bytes 16000000 | tf_op jit(solution)/shard_map/attend_tail/pallas_call | solution.py:264
  64.6 0.0 collective-permute-done.3
  64.6 1.1 %collective-permute-done.4 = bf16[320,576]{1,0:T(8,128)(2,1)S(1)} collective-permute-done((bf16[320,576]{1,0:T(8,128)(2,1)S(1)}, bf16[320,576]{1,0:T(8,128)(2,1)S(1)}, u32[]{:S(2)}, u32[]{:S(2)}) %collective-permute-start.4) | collective-permute-done | bytes 368672 | tf_op jit(solution)/shard_map/ppermute | solution.py:280
  65.7 0.9 %add_convert_fusion = bf16[320,576]{1,0:T(8,128)(2,1)} fusion(bf16[320,576]{1,0:T(8,128)(2,1)S(1)} %collective-permute-done.4, f32[320,576]{1,0:T(8,128)S(1)} %attend_tail.1, bf16[320,576]{1,0:T(8,128)(2,1)S(1)} %collective-permute-done.3), kind=kLoop, calls=%fused_computation | loop fusion | flops 921600 | bytes 1843200 | tf_op jit(solution)/shard_map/convert_element_type | solution.py:305
  (9 shorter events, 0.0 us)
Async XLA Ops:
  0.6 14.4 %collective-permute-start = (bf16[320,576]{1,0:T(8,128)(2,1)}, bf16[320,576]{1,0:T(8,128)(2,1)S(1)}, u32[]{:S(2)}, u32[]{:S(2)}) collective-permute-start(bf16[320,576]{1,0:T(8,128)(2,1)} %own.3), channel_id=1, source_target_pairs={{63,0},{0,1},{1,2},{2,3},{3,4},{4,5},{5,6},{6,7},{7,8},{8,9},{9,10... | collective-permute-start | bytes 1105928 | tf_op jit(solution)/shard_map/ppermute | solution.py:280
  0.7 17.2 %collective-permute-start.1 = (bf16[320,576]{1,0:T(8,128)(2,1)}, bf16[320,576]{1,0:T(8,128)(2,1)S(1)}, u32[]{:S(2)}, u32[]{:S(2)}) collective-permute-start(bf16[320,576]{1,0:T(8,128)(2,1)} %own.3), channel_id=1, source_target_pairs={{62,0},{0,2},{2,4},{4,6},{6,8},{8,10},{10,12},{12,14},{14,16},{16,... | collective-permute-start | bytes 1105928 | tf_op jit(solution)/shard_map/ppermute | solution.py:280
  4.6 1.6 %copy-start = (bf16[512,2048]{1,0:T(8,128)(2,1)S(1)}, bf16[512,2048]{1,0:T(8,128)(2,1)}, u32[]{:S(2)}) copy-start(bf16[512,2048]{1,0:T(8,128)(2,1)} %wk_ref.5) | copy-start | bytes 6291460
  6.2 1.6 %copy-start.2 = (bf16[512,2048]{1,0:T(8,128)(2,1)S(1)}, bf16[512,2048]{1,0:T(8,128)(2,1)}, u32[]{:S(2)}) copy-start(bf16[512,2048]{1,0:T(8,128)(2,1)} %wv_ref.5) | copy-start | bytes 6291460
  7.8 1.0 %copy-start.3 = (bf16[320,576]{1,0:T(8,128)(2,1)S(1)}, bf16[320,576]{1,0:T(8,128)(2,1)}, u32[]{:S(2)}) copy-start(bf16[320,576]{1,0:T(8,128)(2,1)} %own.3) | copy-start | bytes 1105924
  8.8 7.6 %copy-start.7 = (s32[128]{0:T(128)S(1)}, s32[128]{0:T(128)}, u32[]{:S(2)}) copy-start(s32[128]{0:T(128)} %param.11) | copy-start | bytes 1540
  8.8 9.1 %copy-start.4 = (bf16[320,576]{1,0:T(8,128)(2,1)S(1)}, bf16[320,576]{1,0:T(8,128)(2,1)}, u32[]{:S(2)}) copy-start(bf16[320,576]{1,0:T(8,128)(2,1)} %own.3) | copy-start | bytes 1105924
  8.8 9.1 %copy-start.6 = (bf16[320,2048]{1,0:T(8,128)(2,1)S(1)}, bf16[320,2048]{1,0:T(8,128)(2,1)}, u32[]{:S(2)}) copy-start(bf16[320,2048]{1,0:T(8,128)(2,1)} %do_ref.1) | copy-start | bytes 3932164
  15.0 2.8 %collective-permute-start.2 = (bf16[320,576]{1,0:T(8,128)(2,1)S(1)}, bf16[320,576]{1,0:T(8,128)(2,1)S(1)}, u32[]{:S(2)}, u32[]{:S(2)}) collective-permute-start(bf16[320,576]{1,0:T(8,128)(2,1)S(1)} %collective-permute-done.near), channel_id=1, source_target_pairs={{0,1},{2,3},{4,5},{6,7},{8,9},{10,11},{12,13},{14,15},{16,17},{18,... | collective-permute-start | bytes 1105928 | tf_op jit(solution)/shard_map/ppermute | solution.py:285
  16.7 37.2 %copy-start.1 = (bf16[512,2048]{1,0:T(8,128)(2,1)S(1)}, bf16[512,2048]{1,0:T(8,128)(2,1)}, u32[]{:S(2)}) copy-start(bf16[512,2048]{1,0:T(8,128)(2,1)} %wk_ref.5) | copy-start | bytes 6291460
  16.7 37.2 %copy-start.5 = (bf16[320,3072]{1,0:T(8,128)(2,1)S(1)}, bf16[320,3072]{1,0:T(8,128)(2,1)}, u32[]{:S(2)}) copy-start(bf16[320,3072]{1,0:T(8,128)(2,1)} %q_ref.3) | copy-start | bytes 5898244
  47.7 16.9 %collective-permute-start.3 = (bf16[320,576]{1,0:T(8,128)(2,1)S(1)}, bf16[320,576]{1,0:T(8,128)(2,1)S(1)}, u32[]{:S(2)}, u32[]{:S(2)}) collective-permute-start(bf16[320,576]{1,0:T(8,128)(2,1)S(1)} %get-tuple-element.19), channel_id=1, source_target_pairs={{1,0},{2,1},{3,2},{4,3},{5,4},{6,5},{7,6},{8,7},{9,8},{10,9},{11,1... | collective-permute-start | bytes 1105928 | tf_op jit(solution)/shard_map/ppermute | solution.py:280
  51.8 13.8 %collective-permute-start.4 = (bf16[320,576]{1,0:T(8,128)(2,1)S(1)}, bf16[320,576]{1,0:T(8,128)(2,1)S(1)}, u32[]{:S(2)}, u32[]{:S(2)}) collective-permute-start(bf16[320,576]{1,0:T(8,128)(2,1)S(1)} %get-tuple-element.20), channel_id=1, source_target_pairs={{2,0},{3,1},{4,2},{5,3},{6,4},{7,5},{8,6},{9,7},{10,8},{11,9},{12,... | collective-permute-start | bytes 1105928 | tf_op jit(solution)/shard_map/ppermute | solution.py:280

commit v4 on v3

--- a/solution.py
+++ b/solution.py
@@ -60,10 +60,16 @@
 
 
 def keys_body(own, wk_ref, wv_ref, kv_ref):
-    w = jnp.concatenate([head_weights(wk_ref, wv_ref, h) for h in range(2)], 1)
+    count = kv_ref.shape[0]
+    w = jnp.concatenate([head_weights(wk_ref, wv_ref, h) for h in range(count)], 1)
     kv = dot(own[:, :LATENT], w).astype(BF)
-    for h in range(2):
+    for h in range(count):
         kv_ref[h] = kv[:, h * 256 : (h + 1) * 256]
+
+
+def pair_weights(wk_ref, wv_ref, j):
+    cols = slice(j * 2 * NOPE, (j + 1) * 2 * NOPE)
+    return jnp.concatenate([wk_ref[:, cols], wv_ref[:, cols]], 1)
 
 
 def main_body(spans, q_ref, do_ref, own, near, far_a, far_b, wk_ref, wv_ref, okv_ref,
@@ -146,9 +152,36 @@
     rope_t[...] += dk1[NOPE:]
     dk1 = dk1[:NOPE].astype(BF)
     dq1 = (dot_rows(ds1, k1) * SCALE).astype(BF)
-    dq_ref[:, 0*DQ:(1+1)*DQ] = jnp.concatenate([dq0, dq1], 1)
-    held_w[...] = jnp.concatenate([wk_ref[...], wv_ref[...]], 1)
-    held_d[...] = jnp.concatenate([dk0, dk1, dv0, dv1], 0)
+    dq_ref[:, 0*DQ:2*DQ] = jnp.concatenate([dq0, dq1], 1)
+    k2, v2 = project(2)
+    k3, v3 = project(3)
+    s2 = score(2, k2)
+    s3 = score(3, k3)
+    e2 = soften(s2)
+    w01 = pair_weights(wk_ref, wv_ref, 0)
+    d01 = jnp.concatenate([dk0, dk1, dv0, dv1], 0)
+    acc_t[: LATENT // 2] += dot(w01[: LATENT // 2], d01)
+    dos2, delta2 = attend(2, e2, v2)
+    e3 = soften(s3)
+    acc_t[LATENT // 2 :] += dot(w01[LATENT // 2 :], d01)
+    dp2 = dot_nt(dos2, v2)
+    dos3, delta3 = attend(3, e3, v3)
+    ds2 = dscores(2, e2, dp2, delta2)
+    dp3 = dot_nt(dos3, v3)
+    dv2 = dot_tn(dos2, e2[:, :width]).astype(BF)
+    dk2 = dot_tn(q_head(q_ref, 2), ds2[:, :width]) * SCALE
+    rope_t[...] += dk2[NOPE:]
+    dk2 = dk2[:NOPE].astype(BF)
+    dq2 = (dot_rows(ds2, k2) * SCALE).astype(BF)
+    ds3 = dscores(3, e3, dp3, delta3)
+    dv3 = dot_tn(dos3, e3[:, :width]).astype(BF)
+    dk3 = dot_tn(q_head(q_ref, 3), ds3[:, :width]) * SCALE
+    rope_t[...] += dk3[NOPE:]
+    dk3 = dk3[:NOPE].astype(BF)
+    dq3 = (dot_rows(ds3, k3) * SCALE).astype(BF)
+    dq_ref[:, 2*DQ:4*DQ] = jnp.concatenate([dq2, dq3], 1)
+    held_w[...] = pair_weights(wk_ref, wv_ref, 1)
+    held_d[...] = jnp.concatenate([dk2, dk3, dv2, dv3], 0)
 
     @pl.when(p == pl.num_programs(0) - 1)
     def _():
@@ -159,18 +192,20 @@
         tf_ref[:, LATENT:] = rope_t[:, rows:].astype(BF).T
 
 
-def tail_body(q_ref, dos_ref, wk_ref, wv_ref, ds_ref, oe_ref, t_ref, acc_t, rope_t):
+def tail_body(q_ref, dos_ref, wk_ref, wv_ref, ds_ref, oe_ref, t_ref, acc_t, rope_t, held_d, held_w):
     p = pl.program_id(0)
+    count = ds_ref.shape[0]
 
     @pl.when(p == 0)
     def _():
         acc_t[...] = jnp.zeros_like(acc_t)
         rope_t[...] = jnp.zeros_like(rope_t)
-
-    heads = range(2)
-    dvs = [dot_tn(v_head(dos_ref, h), oe_ref[h]).astype(BF) for h in heads]
-    dks = [dot_tn(q_head(q_ref, h), ds_ref[h]) * SCALE for h in heads]
-    rope_t[...] += dks[0][NOPE:] + dks[1][NOPE:]
+        held_d[...] = jnp.zeros_like(held_d)
+        held_w[...] = jnp.zeros_like(held_w)
+
+    dvs = [dot_tn(v_head(dos_ref, h), oe_ref[h]).astype(BF) for h in range(count)]
+    dks = [dot_tn(q_head(q_ref, h), ds_ref[h]) * SCALE for h in range(count)]
+    rope_t[...] += sum(dk[NOPE:] for dk in dks)
     w = jnp.concatenate([wk_ref[...], wv_ref[...]], 1)
     acc_t[...] += dot(w, jnp.concatenate([dk[:NOPE].astype(BF) for dk in dks] + dvs, 0))
 
@@ -208,9 +243,9 @@
     rows = own.shape[0]
     return pl.pallas_call(
         keys_body,
-        grid=(HEADS // 2,),
-        in_specs=[whole(own), columns(LATENT, 256), columns(LATENT, 256)],
-        out_specs=pairs(rows, 256),
+        grid=(HEADS // 4,),
+        in_specs=[whole(own), columns(LATENT, 4 * NOPE), columns(LATENT, 4 * NOPE)],
+        out_specs=heads_block(4, rows, 256),
         out_shape=shape(HEADS, rows, 256),
         compiler_params=params(),
         cost_estimate=cost(7 * 10**8, 8 * 10**6),
@@ -229,11 +264,11 @@
         main_body,
         grid_spec=pltpu.PrefetchScalarGridSpec(
             num_scalar_prefetch=1,
-            grid=(HEADS // 2,),
-            in_specs=[columns(rows, 2 * DQ), columns(rows, 2 * VDIM), whole(own), whole(near), whole(near), whole(near),
-                      columns(LATENT, 2 * 128), columns(LATENT, 2 * 128), heads_block(2, rows, 256)],
-            out_specs=[columns(rows, 2 * VDIM), columns(rows, 2 * DQ), heads_block(2, rows, rows), heads_block(2, rows, rows),
-                       columns(rows, 2 * VDIM), whole(near), whole(near)],
+            grid=(HEADS // 4,),
+            in_specs=[columns(rows, 4 * DQ), columns(rows, 4 * VDIM), whole(own), whole(near), whole(near), whole(near),
+                      columns(LATENT, 4 * NOPE), columns(LATENT, 4 * NOPE), heads_block(4, rows, 256)],
+            out_specs=[columns(rows, 4 * VDIM), columns(rows, 4 * DQ), heads_block(4, rows, rows), heads_block(4, rows, rows),
+                       columns(rows, 4 * VDIM), whole(near), whole(near)],
             scratch_shapes=[
                 pltpu.VMEM((rows, rows), F32),
                 pltpu.VMEM((LATENT, 2 * rows), F32),
@@ -263,11 +298,12 @@
     rows = q.shape[0]
     return pl.pallas_call(
         tail_body,
-        grid=(HEADS // 2,),
-        in_specs=[columns(rows, 2 * DQ), columns(rows, 2 * VDIM), columns(LATENT, 256), columns(LATENT, 256),
-                  pairs(rows, rows), pairs(rows, rows)],
+        grid=(HEADS // 4,),
+        in_specs=[columns(rows, 4 * DQ), columns(rows, 4 * VDIM), columns(LATENT, 4 * NOPE), columns(LATENT, 4 * NOPE),
+                  heads_block(4, rows, rows), heads_block(4, rows, rows)],
         out_specs=whole(own),
-        scratch_shapes=[pltpu.VMEM((LATENT, rows), F32), pltpu.VMEM((ROPE, rows), F32)],
+        scratch_shapes=[pltpu.VMEM((LATENT, rows), F32), pltpu.VMEM((ROPE, rows), F32),
+                        pltpu.VMEM((8 * NOPE, rows), BF), pltpu.VMEM((LATENT, 8 * NOPE), BF)],
         out_shape=shape(*own.shape, dtype=F32),
         compiler_params=params(),
         cost_estimate=cost(3 * 10**9, 16 * 10**6),

time: 67 us -> 64.6 us (0.964)
  Pallas kernels: 45.6 us -> 40.9 us
  waiting for transfers between devices: 3.39 us -> 7.38 us
  starting transfers between devices: 11.5 us -> 9.92 us
    pallas_call x2, Pallas kernels: 15.8 us -> 11.8 us  [the longest x1 8.26 us: call_tail(): pl.pallas_call(tail_body, grid=(HEADS // 4,), in_specs=[columns(rows, 4 *...]
    ppermute x4, waiting for transfers between devices: 3.39 us -> 7.38 us  [routed(): lax.ppermute(block, 'ctx', [((i - distance) % n, i) for i in range(0, n,...]
    ppermute x4, starting transfers between devices: 10.2 us -> 8.61 us  [routed(): lax.ppermute(block, 'ctx', [((i - distance) % n, i) for i in range(0, n,...]
  transfers between devices with their start and end apart: 5 -> 5, of which waited for: 3 -> 3; matrix products, arithmetic and copies ran while one was open for 0% -> 0% of each run, Pallas kernels for 24% -> 18%
where the time goes in v4:
time: 64.6 us; the launch traced here: 64.3 us
  Pallas kernels  40.9 us (63%)
  starting transfers between devices  9.92 us (15%)
  waiting for transfers between devices  7.38 us (11%)
  local copies, waits for them, and re-layouts  4.34 us (7%)
  other arithmetic  0.95 us (1%)
  between operations  0.78 us (1%)
    pallas_call x1, Pallas kernels, call_main(): pl.pallas_call(main_body, grid_spec=pltpu.PrefetchScalarGridSpec(num_scal...  29.1 us
    ppermute x4, starting transfers between devices, routed(): lax.ppermute(block, 'ctx', [((i - distance) % n, i) for i in range(0, n,...  8.61 us
    pallas_call x1, Pallas kernels, call_tail(): pl.pallas_call(tail_body, grid=(HEADS // 4,), in_specs=[columns(rows, 4 *...  8.26 us
    ppermute x4, waiting for transfers between devices, routed(): lax.ppermute(block, 'ctx', [((i - distance) % n, i) for i in range(0, n,...  7.38 us
    unnamed x16, local copies, waits for them, and re-layouts  4.2 us
    pallas_call x1, Pallas kernels, call_keys(): pl.pallas_call(keys_body, grid=(HEADS // 4,), in_specs=[whole(own), colum...  3.55 us
    ppermute x1, starting transfers between devices, to_other_core(): return lax.ppermute(block, 'ctx', [(i, i + 1) for i in range(0, n, 2)])  1.3 us
  transfers between devices with their start and end apart: 5, of which 3 were waited for; matrix products, arithmetic and copies ran while one was open for 0% of the time, Pallas kernels for 18%

profile of v4, /device:TPU:0, one launch (start us, length us, event | category | flops | bytes accessed | tf_op | source)
XLA Modules:
  0.0 64.3 jit_solution(10599071820503522400)
XLA Ops:
  0.6 0.1 collective-permute-start
  0.7 3.9 %collective-permute-start.1 = (bf16[320,576]{1,0:T(8,128)(2,1)}, bf16[320,576]{1,0:T(8,128)(2,1)S(1)}, u32[]{:S(2)}, u32[]{:S(2)}) collective-permute-start(bf16[320,576]{1,0:T(8,128)(2,1)} %own.3), channel_id=1, source_target_pairs={{62,0},{0,2},{2,4},{4,6},{6,8},{8,10},{10,12},{12,14},{14,16},{16,... | collective-permute-start | bytes 1105928 | tf_op jit(solution)/shard_map/ppermute | solution.py:316
  4.6 0.0 copy-start
  4.6 1.6 %copy-done = bf16[512,2048]{1,0:T(8,128)(2,1)S(1)} copy-done((bf16[512,2048]{1,0:T(8,128)(2,1)S(1)}, bf16[512,2048]{1,0:T(8,128)(2,1)}, u32[]{:S(2)}) %copy-start) | copy-done | bytes 2097176
  6.2 1.6 %copy-done.2 = bf16[512,2048]{1,0:T(8,128)(2,1)S(1)} copy-done((bf16[512,2048]{1,0:T(8,128)(2,1)S(1)}, bf16[512,2048]{1,0:T(8,128)(2,1)}, u32[]{:S(2)}) %copy-start.2) | copy-done | bytes 2097176
  7.8 1.0 %copy-done.3 = bf16[320,576]{1,0:T(8,128)(2,1)S(1)} copy-done((bf16[320,576]{1,0:T(8,128)(2,1)S(1)}, bf16[320,576]{1,0:T(8,128)(2,1)}, u32[]{:S(2)}) %copy-start.3) | copy-done | bytes 368664
  8.8 3.6 %project_keys.1.okv_ref = bf16[16,320,256]{2,1,0:T(8,128)(2,1)} custom-call(bf16[320,576]{1,0:T(8,128)(2,1)S(1)} %copy-done.3, bf16[512,2048]{1,0:T(8,128)(2,1)S(1)} %copy-done, bf16[512,2048]{1,0:T(8,128)(2,1)S(1)} %copy-done.2), custom_call_target="tpu_custom_call" | custom-call | flops 1400000000 | bytes 8000000 | tf_op jit(solution)/shard_map/project_keys/pallas_call | solution.py:244
  12.4 2.7 %collective-permute-done.near = bf16[320,576]{1,0:T(8,128)(2,1)S(1)} collective-permute-done((bf16[320,576]{1,0:T(8,128)(2,1)}, bf16[320,576]{1,0:T(8,128)(2,1)S(1)}, u32[]{:S(2)}, u32[]{:S(2)}) %collective-permute-start) | collective-permute-done | bytes 368672 | tf_op jit(solution)/shard_map/ppermute | solution.py:316
  15.0 1.3 %collective-permute-start.2 = (bf16[320,576]{1,0:T(8,128)(2,1)S(1)}, bf16[320,576]{1,0:T(8,128)(2,1)S(1)}, u32[]{:S(2)}, u32[]{:S(2)}) collective-permute-start(bf16[320,576]{1,0:T(8,128)(2,1)S(1)} %collective-permute-done.near), channel_id=1, source_target_pairs={{0,1},{2,3},{4,5},{6,7},{8,9},{10,11},{12,13},{14,15},{16,17},{18,... | collective-permute-start | bytes 1105928 | tf_op jit(solution)/shard_map/ppermute | solution.py:321
  16.4 0.0 copy-done.7
  16.4 0.1 reshape.9
  16.6 0.1 pad_add_fusion.spans
  16.7 1.2 %collective-permute-done.1.far_a = bf16[320,576]{1,0:T(8,128)(2,1)S(1)} collective-permute-done((bf16[320,576]{1,0:T(8,128)(2,1)}, bf16[320,576]{1,0:T(8,128)(2,1)S(1)}, u32[]{:S(2)}, u32[]{:S(2)}) %collective-permute-start.1) | collective-permute-done | bytes 368672 | tf_op jit(solution)/shard_map/ppermute | solution.py:316
  17.9 0.0 collective-permute-done.2.far_b
  17.9 0.0 copy-done.4
  17.9 0.0 copy-done.6
  17.9 29.1 %attend_main.1 = (bf16[320,2048]{1,0:T(8,128)(2,1)}, bf16[320,3072]{1,0:T(8,128)(2,1)}, bf16[16,320,320]{2,1,0:T(8,128)(2,1)}, bf16[16,320,320]{2,1,0:T(8,128)(2...) custom-call(s32[6]{0:T(128)S(1)} %pad_add_fusion.spans, ...), custom_call_target="tpu_custom_call" | custom-call | flops 17999998976 | bytes 35000000 | tf_op jit(solution)/shard_map/attend_main/pallas_call | solution.py:263
  47.0 2.6 %collective-permute-start.3 = (bf16[320,576]{1,0:T(8,128)(2,1)S(1)}, bf16[320,576]{1,0:T(8,128)(2,1)S(1)}, u32[]{:S(2)}, u32[]{:S(2)}) collective-permute-start(bf16[320,576]{1,0:T(8,128)(2,1)S(1)} %get-tuple-element.19), channel_id=1, source_target_pairs={{1,0},{2,1},{3,2},{4,3},{5,4},{6,5},{7,6},{8,7},{9,8},{10,9},{11,1... | collective-permute-start | bytes 1105928 | tf_op jit(solution)/shard_map/ppermute | solution.py:316
  49.6 2.0 %collective-permute-start.4 = (bf16[320,576]{1,0:T(8,128)(2,1)S(1)}, bf16[320,576]{1,0:T(8,128)(2,1)S(1)}, u32[]{:S(2)}, u32[]{:S(2)}) collective-permute-start(bf16[320,576]{1,0:T(8,128)(2,1)S(1)} %get-tuple-element.20), channel_id=1, source_target_pairs={{2,0},{3,1},{4,2},{5,3},{6,4},{7,5},{8,6},{9,7},{10,8},{11,9},{12,... | collective-permute-start | bytes 1105928 | tf_op jit(solution)/shard_map/ppermute | solution.py:316
  51.6 0.0 copy-done.1
  51.6 8.3 %attend_tail.1 = f32[320,576]{1,0:T(8,128)S(1)} custom-call(bf16[320,3072]{1,0:T(8,128)(2,1)S(1)} %copy-done.5, bf16[320,2048]{1,0:T(8,128)(2,1)S(1)} %get-tuple-element.16.dos_ref, bf16[512,2048]{1,0:T(8,128)(2,1)S(1)} %copy-done.1, bf16[512,2048]{1,0:T(8,128)(2,1)} %wv_ref.5, bf16[16,320,320]{2,1,0:T(8,128)(2,1)} %get-tuple-element.17.ds_ref, ...), custom_call_target="tpu_custom_call" | custom-call | flops 6000000000 | bytes 16000000 | tf_op jit(solution)/shard_map/attend_tail/pallas_call | solution.py:299
  59.9 0.0 collective-permute-done.3
  59.9 3.5 %collective-permute-done.4 = bf16[320,576]{1,0:T(8,128)(2,1)S(1)} collective-permute-done((bf16[320,576]{1,0:T(8,128)(2,1)S(1)}, bf16[320,576]{1,0:T(8,128)(2,1)S(1)}, u32[]{:S(2)}, u32[]{:S(2)}) %collective-permute-start.4) | collective-permute-done | bytes 368672 | tf_op jit(solution)/shard_map/ppermute | solution.py:316
  63.4 0.9 %add_convert_fusion = bf16[320,576]{1,0:T(8,128)(2,1)} fusion(bf16[320,576]{1,0:T(8,128)(2,1)S(1)} %collective-permute-done.4, f32[320,576]{1,0:T(8,128)S(1)} %attend_tail.1, bf16[320,576]{1,0:T(8,128)(2,1)S(1)} %collective-permute-done.3), kind=kLoop, calls=%fused_computation | loop fusion | flops 921600 | bytes 1843200 | tf_op jit(solution)/shard_map/convert_element_type | solution.py:341
  (9 shorter events, 0.0 us)
Async XLA Ops:
  0.6 14.4 %collective-permute-start = (bf16[320,576]{1,0:T(8,128)(2,1)}, bf16[320,576]{1,0:T(8,128)(2,1)S(1)}, u32[]{:S(2)}, u32[]{:S(2)}) collective-permute-start(bf16[320,576]{1,0:T(8,128)(2,1)} %own.3), channel_id=1, source_target_pairs={{63,0},{0,1},{1,2},{2,3},{3,4},{4,5},{5,6},{6,7},{7,8},{8,9},{9,10... | collective-permute-start | bytes 1105928 | tf_op jit(solution)/shard_map/ppermute | solution.py:316
  0.7 17.2 %collective-permute-start.1 = (bf16[320,576]{1,0:T(8,128)(2,1)}, bf16[320,576]{1,0:T(8,128)(2,1)S(1)}, u32[]{:S(2)}, u32[]{:S(2)}) collective-permute-start(bf16[320,576]{1,0:T(8,128)(2,1)} %own.3), channel_id=1, source_target_pairs={{62,0},{0,2},{2,4},{4,6},{6,8},{8,10},{10,12},{12,14},{14,16},{16,... | collective-permute-start | bytes 1105928 | tf_op jit(solution)/shard_map/ppermute | solution.py:316
  4.6 1.6 %copy-start = (bf16[512,2048]{1,0:T(8,128)(2,1)S(1)}, bf16[512,2048]{1,0:T(8,128)(2,1)}, u32[]{:S(2)}) copy-start(bf16[512,2048]{1,0:T(8,128)(2,1)} %wk_ref.5) | copy-start | bytes 6291460
  6.2 1.6 %copy-start.2 = (bf16[512,2048]{1,0:T(8,128)(2,1)S(1)}, bf16[512,2048]{1,0:T(8,128)(2,1)}, u32[]{:S(2)}) copy-start(bf16[512,2048]{1,0:T(8,128)(2,1)} %wv_ref.5) | copy-start | bytes 6291460
  7.8 1.0 %copy-start.3 = (bf16[320,576]{1,0:T(8,128)(2,1)S(1)}, bf16[320,576]{1,0:T(8,128)(2,1)}, u32[]{:S(2)}) copy-start(bf16[320,576]{1,0:T(8,128)(2,1)} %own.3) | copy-start | bytes 1105924
  8.8 7.6 %copy-start.7 = (s32[128]{0:T(128)S(1)}, s32[128]{0:T(128)}, u32[]{:S(2)}) copy-start(s32[128]{0:T(128)} %param.11) | copy-start | bytes 1540
  8.8 9.1 %copy-start.4 = (bf16[320,576]{1,0:T(8,128)(2,1)S(1)}, bf16[320,576]{1,0:T(8,128)(2,1)}, u32[]{:S(2)}) copy-start(bf16[320,576]{1,0:T(8,128)(2,1)} %own.3) | copy-start | bytes 1105924
  8.8 9.1 %copy-start.6 = (bf16[320,2048]{1,0:T(8,128)(2,1)S(1)}, bf16[320,2048]{1,0:T(8,128)(2,1)}, u32[]{:S(2)}) copy-start(bf16[320,2048]{1,0:T(8,128)(2,1)} %do_ref.1) | copy-start | bytes 3932164
  15.0 2.8 %collective-permute-start.2 = (bf16[320,576]{1,0:T(8,128)(2,1)S(1)}, bf16[320,576]{1,0:T(8,128)(2,1)S(1)}, u32[]{:S(2)}, u32[]{:S(2)}) collective-permute-start(bf16[320,576]{1,0:T(8,128)(2,1)S(1)} %collective-permute-done.near), channel_id=1, source_target_pairs={{0,1},{2,3},{4,5},{6,7},{8,9},{10,11},{12,13},{14,15},{16,17},{18,... | collective-permute-start | bytes 1105928 | tf_op jit(solution)/shard_map/ppermute | solution.py:321
  16.7 35.0 %copy-start.1 = (bf16[512,2048]{1,0:T(8,128)(2,1)S(1)}, bf16[512,2048]{1,0:T(8,128)(2,1)}, u32[]{:S(2)}) copy-start(bf16[512,2048]{1,0:T(8,128)(2,1)} %wk_ref.5) | copy-start | bytes 6291460
  16.7 35.0 %copy-start.5 = (bf16[320,3072]{1,0:T(8,128)(2,1)S(1)}, bf16[320,3072]{1,0:T(8,128)(2,1)}, u32[]{:S(2)}) copy-start(bf16[320,3072]{1,0:T(8,128)(2,1)} %q_ref.3) | copy-start | bytes 5898244
  47.0 12.9 %collective-permute-start.3 = (bf16[320,576]{1,0:T(8,128)(2,1)S(1)}, bf16[320,576]{1,0:T(8,128)(2,1)S(1)}, u32[]{:S(2)}, u32[]{:S(2)}) collective-permute-start(bf16[320,576]{1,0:T(8,128)(2,1)S(1)} %get-tuple-element.19), channel_id=1, source_target_pairs={{1,0},{2,1},{3,2},{4,3},{5,4},{6,5},{7,6},{8,7},{9,8},{10,9},{11,1... | collective-permute-start | bytes 1105928 | tf_op jit(solution)/shard_map/ppermute | solution.py:316
  49.6 13.8 %collective-permute-start.4 = (bf16[320,576]{1,0:T(8,128)(2,1)S(1)}, bf16[320,576]{1,0:T(8,128)(2,1)S(1)}, u32[]{:S(2)}, u32[]{:S(2)}) collective-permute-start(bf16[320,576]{1,0:T(8,128)(2,1)S(1)} %get-tuple-element.20), channel_id=1, source_target_pairs={{2,0},{3,1},{4,2},{5,3},{6,4},{7,5},{8,6},{9,7},{10,8},{11,9},{12,... | collective-permute-start | bytes 1105928 | tf_op jit(solution)/shard_map/ppermute | solution.py:316

commit v5 on v4

--- a/solution.py
+++ b/solution.py
@@ -334,10 +334,13 @@
     out, dq, ds, oe, dos, t_near, t_far = call_main(
         spans, queries, grad_out, latent, near, far_a, far_b, w_key_up, w_value_up, okv
     )
-    from_far = routed(t_far, -2)
-    from_near = routed(t_near, -1)
+    swapped = lax.ppermute(t_near, "ctx", [(i, i ^ 1) for i in range(n)])
+    odd = me % 2 == 1
+    none = jnp.zeros_like(swapped)
+    passed_on, ds = lax.optimization_barrier((t_far + jnp.where(odd, swapped, none), ds))
+    arrived = routed(passed_on, -2)
     own_term = call_tail(queries, dos, latent, w_key_up, w_value_up, ds, oe)
-    total = own_term + from_near.astype(F32) + from_far.astype(F32)
+    total = own_term + arrived.astype(F32) + jnp.where(odd, none, swapped).astype(F32)
     return out, dq, total.astype(BF)
 
 

time: 64.6 us -> 69.2 us (1.071); the launches traced: 64.3 us -> 68 us
  local copies, waits for them, and re-layouts: 4.34 us -> 11.4 us
  waiting for transfers between devices: 7.38 us -> 5.14 us
  starting transfers between devices: 9.92 us -> 8.47 us
    unnamed x16 -> x24, local copies, waits for them, and re-layouts: 4.2 us -> 11.3 us
    ppermute x4 -> x3, waiting for transfers between devices: 7.38 us -> 3.18 us  [routed(): lax.ppermute(block, 'ctx', [((i - distance) % n, i) for i in range(0, n,...]
    ppermute x4 -> x3, starting transfers between devices: 8.61 us -> 6.42 us  [routed(): lax.ppermute(block, 'ctx', [((i - distance) % n, i) for i in range(0, n,...]
    ppermute x0 -> x1, waiting for transfers between devices: none -> 1.95 us  [on_device(): swapped = lax.ppermute(t_near, 'ctx', [(i, i ^ 1) for i in range(n)])]
    ppermute x1, starting transfers between devices: 1.3 us -> 2.05 us  [to_other_core(): return lax.ppermute(block, 'ctx', [(i, i + 1) for i in range(0, n, 2)])]
  transfers between devices with their start and end apart: 5 -> 5, of which waited for: 3 -> 3; matrix products, arithmetic and copies ran while one was open for 0% -> 0% of each run, Pallas kernels for 18% -> 17%
where the time goes in v5:
time: 69.2 us; the launch traced here: 68 us
  Pallas kernels  41.2 us (60%)
  local copies, waits for them, and re-layouts  11.4 us (16%)
  starting transfers between devices  8.47 us (12%)
  waiting for transfers between devices  5.14 us (7%)
  other arithmetic  1.04 us (2%)
  between operations  0.74 us (1%)
    pallas_call x1, Pallas kernels, call_main(): pl.pallas_call(main_body, grid_spec=pltpu.PrefetchScalarGridSpec(num_scal...  29.4 us
    unnamed x24, local copies, waits for them, and re-layouts  11.3 us
    pallas_call x1, Pallas kernels, call_tail(): pl.pallas_call(tail_body, grid=(HEADS // 4,), in_specs=[columns(rows, 4 *...  8.26 us
    ppermute x3, starting transfers between devices, routed(): lax.ppermute(block, 'ctx', [((i - distance) % n, i) for i in range(0, n,...  6.42 us
    pallas_call x1, Pallas kernels, call_keys(): pl.pallas_call(keys_body, grid=(HEADS // 4,), in_specs=[whole(own), colum...  3.57 us
    ppermute x3, waiting for transfers between devices, routed(): lax.ppermute(block, 'ctx', [((i - distance) % n, i) for i in range(0, n,...  3.18 us
    ppermute x1, starting transfers between devices, to_other_core(): return lax.ppermute(block, 'ctx', [(i, i + 1) for i in range(0, n, 2)])  2.05 us
    ppermute x1, waiting for transfers between devices, on_device(): swapped = lax.ppermute(t_near, 'ctx', [(i, i ^ 1) for i in range(n)])  1.95 us
  transfers between devices with their start and end apart: 5, of which 3 were waited for; matrix products, arithmetic and copies ran while one was open for 0% of the time, Pallas kernels for 17%

profile of v5, /device:TPU:0, one launch (start us, length us, event | category | flops | bytes accessed | tf_op | source)
XLA Modules:
  0.0 68.0 jit_solution(5463096500843492938)
XLA Ops:
  0.6 0.1 collective-permute-start
  0.7 3.9 %collective-permute-start.1 = (bf16[320,576]{1,0:T(8,128)(2,1)}, bf16[320,576]{1,0:T(8,128)(2,1)S(1)}, u32[]{:S(2)}, u32[]{:S(2)}) collective-permute-start(bf16[320,576]{1,0:T(8,128)(2,1)} %own.3), channel_id=1, source_target_pairs={{62,0},{0,2},{2,4},{4,6},{6,8},{8,10},{10,12},{12,14},{14,16},{16,... | collective-permute-start | bytes 1105928 | tf_op jit(solution)/shard_map/ppermute | solution.py:316
  4.6 0.0 copy-start
  4.6 1.6 %copy-done = bf16[512,2048]{1,0:T(8,128)(2,1)S(1)} copy-done((bf16[512,2048]{1,0:T(8,128)(2,1)S(1)}, bf16[512,2048]{1,0:T(8,128)(2,1)}, u32[]{:S(2)}) %copy-start) | copy-done | bytes 2097176
  6.2 1.6 %copy-done.2 = bf16[512,2048]{1,0:T(8,128)(2,1)S(1)} copy-done((bf16[512,2048]{1,0:T(8,128)(2,1)S(1)}, bf16[512,2048]{1,0:T(8,128)(2,1)}, u32[]{:S(2)}) %copy-start.2) | copy-done | bytes 2097176
  7.8 1.0 %copy-done.3 = bf16[320,576]{1,0:T(8,128)(2,1)S(1)} copy-done((bf16[320,576]{1,0:T(8,128)(2,1)S(1)}, bf16[320,576]{1,0:T(8,128)(2,1)}, u32[]{:S(2)}) %copy-start.3) | copy-done | bytes 368664
  8.8 3.6 %project_keys.1.okv_ref = bf16[16,320,256]{2,1,0:T(8,128)(2,1)} custom-call(bf16[320,576]{1,0:T(8,128)(2,1)S(1)} %copy-done.3, bf16[512,2048]{1,0:T(8,128)(2,1)S(1)} %copy-done, bf16[512,2048]{1,0:T(8,128)(2,1)S(1)} %copy-done.2), custom_call_target="tpu_custom_call" | custom-call | flops 1400000000 | bytes 8000000 | tf_op jit(solution)/shard_map/project_keys/pallas_call | solution.py:244
  12.4 2.6 %collective-permute-done.near = bf16[320,576]{1,0:T(8,128)(2,1)S(1)} collective-permute-done((bf16[320,576]{1,0:T(8,128)(2,1)}, bf16[320,576]{1,0:T(8,128)(2,1)S(1)}, u32[]{:S(2)}, u32[]{:S(2)}) %collective-permute-start) | collective-permute-done | bytes 368672 | tf_op jit(solution)/shard_map/ppermute | solution.py:316
  15.0 2.0 %collective-permute-start.2 = (bf16[320,576]{1,0:T(8,128)(2,1)S(1)}, bf16[320,576]{1,0:T(8,128)(2,1)}, u32[]{:S(2)}, u32[]{:S(2)}) collective-permute-start(bf16[320,576]{1,0:T(8,128)(2,1)S(1)} %collective-permute-done.near), channel_id=1, source_target_pairs={{0,1},{2,3},{4,5},{6,7},{8,9},{10,11},{12,13},{14,15},{16,17},{18,... | collective-permute-start | bytes 1105928 | tf_op jit(solution)/shard_map/ppermute | solution.py:321
  17.1 0.1 reshape.9
  17.3 0.1 pad_add_fusion.spans
  17.3 0.5 collective-permute-done.1.far_a
  17.9 0.7 %copy-done.7 = bf16[320,576]{1,0:T(8,128)(2,1)} copy-done((bf16[320,576]{1,0:T(8,128)(2,1)}, bf16[320,576]{1,0:T(8,128)(2,1)S(1)}, u32[]{:S(2)}) %copy-start.7) | copy-done | bytes 368664
  18.6 1.3 %copy-done.6 = bf16[320,2048]{1,0:T(8,128)(2,1)S(1)} copy-done((bf16[320,2048]{1,0:T(8,128)(2,1)S(1)}, bf16[320,2048]{1,0:T(8,128)(2,1)}, u32[]{:S(2)}) %copy-start.6) | copy-done | bytes 1310744
  20.0 1.0 %copy-done.8 = bf16[320,576]{1,0:T(8,128)(2,1)S(1)} copy-done((bf16[320,576]{1,0:T(8,128)(2,1)S(1)}, bf16[320,576]{1,0:T(8,128)(2,1)}, u32[]{:S(2)}) %copy-start.8) | copy-done | bytes 368664
  21.0 29.4 %attend_main.1 = (bf16[320,2048]{1,0:T(8,128)(2,1)}, bf16[320,3072]{1,0:T(8,128)(2,1)}, bf16[16,320,320]{2,1,0:T(8,128)(2,1)}, bf16[16,320,320]{2,1,0:T(8,128)(2...) custom-call(s32[6]{0:T(128)S(1)} %pad_add_fusion.spans, ...), custom_call_target="tpu_custom_call" | custom-call | flops 17999998976 | bytes 35000000 | tf_op jit(solution)/shard_map/attend_main/pallas_call | solution.py:263
  50.3 1.1 %copy-done.9 = bf16[320,2048]{1,0:T(8,128)(2,1)} copy-done((bf16[320,2048]{1,0:T(8,128)(2,1)}, bf16[320,2048]{1,0:T(8,128)(2,1)S(1)}, u32[]{:S(2)}) %copy-start.9) | copy-done | bytes 1310744
  51.5 2.0 %collective-permute-done.3 = bf16[320,576]{1,0:T(8,128)(2,1)S(1)} collective-permute-done((bf16[320,576]{1,0:T(8,128)(2,1)}, bf16[320,576]{1,0:T(8,128)(2,1)S(1)}, u32[]{:S(2)}, u32[]{:S(2)}) %collective-permute-start.3) | collective-permute-done | bytes 368672 | tf_op jit(solution)/shard_map/ppermute | solution.py:337
  53.4 0.1 select_add_fusion
  53.5 2.4 %collective-permute-start.4 = (bf16[320,576]{1,0:T(8,128)(2,1)S(1)}, bf16[320,576]{1,0:T(8,128)(2,1)S(1)}, u32[]{:S(2)}, u32[]{:S(2)}) collective-permute-start(bf16[320,576]{1,0:T(8,128)(2,1)S(1)} %select_add_fusion), channel_id=1, source_target_pairs={{2,0},{3,1},{4,2},{5,3},{6,4},{7,5},{8,6},{9,7},{10,8},{11,9},{12,... | collective-permute-start | bytes 1105928 | tf_op jit(solution)/shard_map/ppermute | solution.py:316
  56.0 1.5 %copy-done.5 = bf16[320,3072]{1,0:T(8,128)(2,1)S(1)} copy-done((bf16[320,3072]{1,0:T(8,128)(2,1)S(1)}, bf16[320,3072]{1,0:T(8,128)(2,1)}, u32[]{:S(2)}) %copy-start.5) | copy-done | bytes 1966104
  57.5 1.3 %copy-done.10 = bf16[320,2048]{1,0:T(8,128)(2,1)S(1)} copy-done((bf16[320,2048]{1,0:T(8,128)(2,1)S(1)}, bf16[320,2048]{1,0:T(8,128)(2,1)}, u32[]{:S(2)}) %copy-start.10) | copy-done | bytes 1310744
  58.8 8.3 %attend_tail.1 = f32[320,576]{1,0:T(8,128)S(1)} custom-call(bf16[320,3072]{1,0:T(8,128)(2,1)S(1)} %copy-done.5, bf16[320,2048]{1,0:T(8,128)(2,1)S(1)} %copy-done.10, bf16[512,2048]{1,0:T(8,128)(2,1)S(1)} %copy-done.1, bf16[512,2048]{1,0:T(8,128)(2,1)} %wv_ref.5, bf16[16,320,320]{2,1,0:T(8,128)(2,1)} %get-tuple-element.22.ds_ref, ...), custom_call_target="tpu_custom_call" | custom-call | flops 6000000000 | bytes 16000000 | tf_op jit(solution)/shard_map/attend_tail/pallas_call | solution.py:299
  67.1 0.9 %add_convert_fusion = bf16[320,576]{1,0:T(8,128)(2,1)} fusion(f32[320,576]{1,0:T(8,128)S(1)} %attend_tail.1, bf16[320,576]{1,0:T(8,128)(2,1)S(1)} %collective-permute-done.4, bf16[320,576]{1,0:T(8,128)(2,1)S(1)} %collective-permute-done.3, pred[]{:T(512)S(6)} %eq.8), kind=kLoop, calls=%fused_computation | loop fusion | flops 1105920 | bytes 1843201 | tf_op jit(solution)/shard_map/convert_element_type | solution.py:344
  (18 shorter events, 0.0 us)
Async XLA Ops:
  0.6 14.4 %collective-permute-start = (bf16[320,576]{1,0:T(8,128)(2,1)}, bf16[320,576]{1,0:T(8,128)(2,1)S(1)}, u32[]{:S(2)}, u32[]{:S(2)}) collective-permute-start(bf16[320,576]{1,0:T(8,128)(2,1)} %own.3), channel_id=1, source_target_pairs={{63,0},{0,1},{1,2},{2,3},{3,4},{4,5},{5,6},{6,7},{7,8},{8,9},{9,10... | collective-permute-start | bytes 1105928 | tf_op jit(solution)/shard_map/ppermute | solution.py:316
  0.7 17.2 %collective-permute-start.1 = (bf16[320,576]{1,0:T(8,128)(2,1)}, bf16[320,576]{1,0:T(8,128)(2,1)S(1)}, u32[]{:S(2)}, u32[]{:S(2)}) collective-permute-start(bf16[320,576]{1,0:T(8,128)(2,1)} %own.3), channel_id=1, source_target_pairs={{62,0},{0,2},{2,4},{4,6},{6,8},{8,10},{10,12},{12,14},{14,16},{16,... | collective-permute-start | bytes 1105928 | tf_op jit(solution)/shard_map/ppermute | solution.py:316
  4.6 1.6 %copy-start = (bf16[512,2048]{1,0:T(8,128)(2,1)S(1)}, bf16[512,2048]{1,0:T(8,128)(2,1)}, u32[]{:S(2)}) copy-start(bf16[512,2048]{1,0:T(8,128)(2,1)} %wk_ref.5) | copy-start | bytes 6291460
  6.2 1.6 %copy-start.2 = (bf16[512,2048]{1,0:T(8,128)(2,1)S(1)}, bf16[512,2048]{1,0:T(8,128)(2,1)}, u32[]{:S(2)}) copy-start(bf16[512,2048]{1,0:T(8,128)(2,1)} %wv_ref.5) | copy-start | bytes 6291460
  7.8 1.0 %copy-start.3 = (bf16[320,576]{1,0:T(8,128)(2,1)S(1)}, bf16[320,576]{1,0:T(8,128)(2,1)}, u32[]{:S(2)}) copy-start(bf16[320,576]{1,0:T(8,128)(2,1)} %own.3) | copy-start | bytes 1105924
  8.8 8.3 %copy-start.11 = (s32[128]{0:T(128)S(1)}, s32[128]{0:T(128)}, u32[]{:S(2)}) copy-start(s32[128]{0:T(128)} %param.11) | copy-start | bytes 1540
  8.8 9.8 %copy-start.4 = (bf16[320,576]{1,0:T(8,128)(2,1)S(1)}, bf16[320,576]{1,0:T(8,128)(2,1)}, u32[]{:S(2)}) copy-start(bf16[320,576]{1,0:T(8,128)(2,1)} %own.3) | copy-start | bytes 1105924
  15.0 3.6 %collective-permute-start.2 = (bf16[320,576]{1,0:T(8,128)(2,1)S(1)}, bf16[320,576]{1,0:T(8,128)(2,1)}, u32[]{:S(2)}, u32[]{:S(2)}) collective-permute-start(bf16[320,576]{1,0:T(8,128)(2,1)S(1)} %collective-permute-done.near), channel_id=1, source_target_pairs={{0,1},{2,3},{4,5},{6,7},{8,9},{10,11},{12,13},{14,15},{16,17},{18,... | collective-permute-start | bytes 1105928 | tf_op jit(solution)/shard_map/ppermute | solution.py:321
  17.3 38.6 %copy-start.1 = (bf16[512,2048]{1,0:T(8,128)(2,1)S(1)}, bf16[512,2048]{1,0:T(8,128)(2,1)}, u32[]{:S(2)}) copy-start(bf16[512,2048]{1,0:T(8,128)(2,1)} %wk_ref.5) | copy-start | bytes 6291460
  17.9 0.8 %copy-start.7 = (bf16[320,576]{1,0:T(8,128)(2,1)}, bf16[320,576]{1,0:T(8,128)(2,1)S(1)}, u32[]{:S(2)}) copy-start(bf16[320,576]{1,0:T(8,128)(2,1)S(1)} %collective-permute-done.1.far_a) | copy-start | bytes 1105924
  18.6 1.3 %copy-start.6 = (bf16[320,2048]{1,0:T(8,128)(2,1)S(1)}, bf16[320,2048]{1,0:T(8,128)(2,1)}, u32[]{:S(2)}) copy-start(bf16[320,2048]{1,0:T(8,128)(2,1)} %do_ref.1) | copy-start | bytes 3932164
  19.9 1.0 %copy-start.8 = (bf16[320,576]{1,0:T(8,128)(2,1)S(1)}, bf16[320,576]{1,0:T(8,128)(2,1)}, u32[]{:S(2)}) copy-start(bf16[320,576]{1,0:T(8,128)(2,1)} %copy-done.7) | copy-start | bytes 1105924
  50.3 1.2 %copy-start.9 = (bf16[320,2048]{1,0:T(8,128)(2,1)}, bf16[320,2048]{1,0:T(8,128)(2,1)S(1)}, u32[]{:S(2)}) copy-start(bf16[320,2048]{1,0:T(8,128)(2,1)S(1)} %get-tuple-element.18.dos_ref) | copy-start | bytes 3932164
  51.5 2.0 %collective-permute-start.3 = (bf16[320,576]{1,0:T(8,128)(2,1)}, bf16[320,576]{1,0:T(8,128)(2,1)S(1)}, u32[]{:S(2)}, u32[]{:S(2)}) collective-permute-start(bf16[320,576]{1,0:T(8,128)(2,1)} %get-tuple-element.20), channel_id=1, source_target_pairs={{0,1},{1,0},{2,3},{3,2},{4,5},{5,4},{6,7},{7,6},{8,9},{9,8},{10,11... | collective-permute-start | bytes 1105928 | tf_op jit(solution)/shard_map/ppermute | solution.py:337
  53.5 13.6 %collective-permute-start.4 = (bf16[320,576]{1,0:T(8,128)(2,1)S(1)}, bf16[320,576]{1,0:T(8,128)(2,1)S(1)}, u32[]{:S(2)}, u32[]{:S(2)}) collective-permute-start(bf16[320,576]{1,0:T(8,128)(2,1)S(1)} %select_add_fusion), channel_id=1, source_target_pairs={{2,0},{3,1},{4,2},{5,3},{6,4},{7,5},{8,6},{9,7},{10,8},{11,9},{12,... | collective-permute-start | bytes 1105928 | tf_op jit(solution)/shard_map/ppermute | solution.py:316
  55.9 1.5 %copy-start.5 = (bf16[320,3072]{1,0:T(8,128)(2,1)S(1)}, bf16[320,3072]{1,0:T(8,128)(2,1)}, u32[]{:S(2)}) copy-start(bf16[320,3072]{1,0:T(8,128)(2,1)} %q_ref.3) | copy-start | bytes 5898244
  57.5 1.3 %copy-start.10 = (bf16[320,2048]{1,0:T(8,128)(2,1)S(1)}, bf16[320,2048]{1,0:T(8,128)(2,1)}, u32[]{:S(2)}) copy-start(bf16[320,2048]{1,0:T(8,128)(2,1)} %copy-done.9) | copy-start | bytes 3932164
